TPU v7x, 32 devices: a whole 2x2x4 slice. The times are simulated.
32 devices in a mesh: member: 2 (over x), node: 16 (over z, y, core).
Axes of the slice: x: 2, y: 2, z: 4, core: 2. Of those that a mesh axis runs over, the one named last changes fastest.
Arguments:
- vertex_embedding_array: bfloat16 [2, 65536, 128], P('member', 'node'), may hold values from -12 to 12
- result_sensitivity: bfloat16 [2, 65536, 128], P('member', 'node'), may hold values from -6 to 6
- hidden_projection: bfloat16 [128, 128], replicated, may hold values from -0.5 to 0.5
- aggregate_projection: bfloat16 [128, 128], replicated, may hold values from -0.5 to 0.5
- aggregate_offset: float32 [128], replicated, may hold values from -3 to 3
- assignment_projection: bfloat16 [16, 32], replicated, may hold values from -1.5 to 1.5
- softmax_sharpness: float32 [8], replicated, may hold values from 0.5 to 2
- state_asking_map: bfloat16 [16, 16], replicated, may hold values from -1.5 to 1.5
- state_lookup_map: bfloat16 [16, 16], replicated, may hold values from -1.5 to 1.5
- state_content_map: bfloat16 [16, 16], replicated, may hold values from -1.5 to 1.5
- result_projection: bfloat16 [128, 128], replicated, may hold values from -0.5 to 0.5
Outputs:
- vertex_sensitivity: float32 [2, 65536, 128], P('member', 'node')
- mid_grad: float32 [128, 128], replicated
- feature_grad: float32 [128, 128], replicated
- bias_grad: float32 [128], replicated
- slice_grad: float32 [16, 32], replicated
- temperature_grad: float32 [8], replicated
- query_grad: float32 [16, 16], replicated
- key_grad: float32 [16, 16], replicated
- value_grad: float32 [16, 16], replicated
- projection_grad: float32 [128, 128], replicated
All inputs are finite; a program needn't handle non-finite values.
Results may differ from a plain program's by a relative error of at most 0.0054.
The roundings to bfloat16 on the way count: a program that leaves them out, or rounds other values in their place, can miss the bound.
Values sent between devices are 32-bit elements; how exact they have to be, the bound alone decides.
A program may use at most 64 MiB of HBM per device.

v0:
```python
import math

import jax
import jax.numpy as jnp
from jax import lax
from jax.sharding import PartitionSpec as P

MODEL_WIDTH = 128
NUM_CHANNELS = 8
D = 16


epsilon = 1e-05


def attend(physical_state_vectors, state_asking_map, state_lookup_map, state_content_map):
    exact_arithmetic_mode = lax.Precision.HIGHEST
    asking_vectors = jnp.einsum(
        "uzi,ib->uzb", physical_state_vectors, state_asking_map, precision=exact_arithmetic_mode
    )
    random_seed_list = jnp.einsum(
        "uzi,ib->uzb", physical_state_vectors, state_lookup_map, precision=exact_arithmetic_mode
    )
    content_vectors = jnp.einsum(
        "uzi,ib->uzb", physical_state_vectors, state_content_map, precision=exact_arithmetic_mode
    )
    assignment_shares = jnp.einsum(
        "hme,hke->hmk", asking_vectors, random_seed_list, precision=exact_arithmetic_mode
    ) / math.sqrt(physical_state_vectors.shape[-1])
    expon = jnp.exp(assignment_shares)
    attention_rows = expon / jnp.sum(expon, -1, keepdims=True)
    return jnp.einsum(
        "lso,log->lsg", attention_rows, content_vectors, precision=exact_arithmetic_mode
    )


def shards(
    vertex_embedding_array,
    result_sensitivity,
    hidden_projection,
    aggregate_projection,
    aggregate_offset,
    assignment_projection,
    softmax_sharpness,
    state_asking_map,
    state_lookup_map,
    state_content_map,
    result_projection,
):
    channel_embedding = vertex_embedding_array[0]
    incoming_sensitivity = result_sensitivity[0]
    mesh_node_rows = channel_embedding.shape[0]
    mid_half = (
        jnp.dot(channel_embedding, hidden_projection, preferred_element_type=jnp.float32)
        .astype(jnp.bfloat16)
        .reshape(mesh_node_rows, NUM_CHANNELS, D)
    )
    feature_halfway = (
        (
            jnp.dot(channel_embedding, aggregate_projection, preferred_element_type=jnp.float32)
            + aggregate_offset
        )
        .astype(jnp.bfloat16)
        .reshape(mesh_node_rows, NUM_CHANNELS, D)
    )
    assignment_shares = jnp.einsum(
        "nhd,dm->nhm", mid_half, assignment_projection, preferred_element_type=jnp.float32
    )
    assignment_energies = assignment_shares / softmax_sharpness[None, :, None]
    expon = jnp.exp(assignment_energies)
    probs = expon / jnp.sum(expon, -1, keepdims=True)
    probability_halfway = probs.astype(jnp.bfloat16)
    pooled_numerator = jnp.einsum(
        "wou,wog->oug", probability_halfway, feature_halfway, preferred_element_type=jnp.float32
    )
    denominator = jnp.sum(probs, 0)
    pooled_numerator, denominator = lax.psum((pooled_numerator, denominator), "node")
    physical_state_vectors = pooled_numerator / (denominator[:, :, None] + epsilon)
    token_out, attend_back = jax.vjp(
        attend,
        physical_state_vectors,
        state_asking_map.astype(jnp.float32),
        state_lookup_map.astype(jnp.float32),
        state_content_map.astype(jnp.float32),
    )
    tokens_halfway = token_out.astype(jnp.bfloat16)
    mixed_half = (
        jnp.einsum(
            "afq,fqx->afx", probability_halfway, tokens_halfway, preferred_element_type=jnp.float32
        )
        .reshape(mesh_node_rows, MODEL_WIDTH)
        .astype(jnp.bfloat16)
    )
    backward_halfway = (
        jnp.dot(incoming_sensitivity, result_projection.T, preferred_element_type=jnp.float32)
        .astype(jnp.bfloat16)
        .reshape(mesh_node_rows, NUM_CHANNELS, D)
    )
    mapping_contribution = jnp.dot(
        mixed_half.T, incoming_sensitivity, preferred_element_type=jnp.float32
    )
    slice_token_gradient = jnp.einsum(
        "wou,wog->oug", probability_halfway, backward_halfway, preferred_element_type=jnp.float32
    )
    slice_token_gradient = lax.psum(slice_token_gradient, "node")
    piece_reverse_derivative, asking_contribution, lookup_contribution, content_contribution = (
        attend_back(slice_token_gradient)
    )
    inverse = 1.0 / (denominator + epsilon)
    numerator_halfway = (piece_reverse_derivative * inverse[:, :, None]).astype(jnp.bfloat16)
    denom_back = -jnp.sum(piece_reverse_derivative * physical_state_vectors, -1) * inverse
    probability_backward = jnp.einsum(
        "yrq,req->yre", backward_halfway, tokens_halfway, preferred_element_type=jnp.float32
    )
    probability_backward = probability_backward + jnp.einsum(
        "yrq,req->yre", feature_halfway, numerator_halfway, preferred_element_type=jnp.float32
    )
    probability_backward = probability_backward + denom_back[None]
    feature_backward = jnp.einsum(
        "afq,fqx->afx", probability_halfway, numerator_halfway, preferred_element_type=jnp.float32
    ).reshape(mesh_node_rows, MODEL_WIDTH)
    shift_term_derivative = jnp.sum(feature_backward, 0)
    feat_back_half = feature_backward.astype(jnp.bfloat16)
    inner = jnp.sum(probs * probability_backward, -1, keepdims=True)
    assignment_energy_adjoint = probs * (probability_backward - inner)
    inverse_spread_derivative = (
        -jnp.sum(assignment_energy_adjoint * assignment_energies, axis=(0, 2)) / softmax_sharpness
    )
    assignment_partial_result = (
        assignment_energy_adjoint / softmax_sharpness[None, :, None]
    ).astype(jnp.bfloat16)
    division_term_derivative = jnp.einsum(
        "nhd,nhm->dm", mid_half, assignment_partial_result, preferred_element_type=jnp.float32
    )
    mid_back_half = (
        jnp.einsum(
            "nhm,dm->nhd",
            assignment_partial_result,
            assignment_projection,
            preferred_element_type=jnp.float32,
        )
        .reshape(mesh_node_rows, MODEL_WIDTH)
        .astype(jnp.bfloat16)
    )
    hidden_contribution = jnp.dot(
        channel_embedding.T, mid_back_half, preferred_element_type=jnp.float32
    )
    channel_contribution = jnp.dot(
        channel_embedding.T, feat_back_half, preferred_element_type=jnp.float32
    )
    vertex_sensitivity = jnp.dot(
        mid_back_half, hidden_projection.T, preferred_element_type=jnp.float32
    ) + jnp.dot(feat_back_half, aggregate_projection.T, preferred_element_type=jnp.float32)
    dominant_summands = (hidden_contribution, channel_contribution, mapping_contribution)
    trailing_summands = (shift_term_derivative, division_term_derivative, inverse_spread_derivative)
    token_terms = (asking_contribution, lookup_contribution, content_contribution)
    piece_totals = lax.psum((token_terms[0], token_terms[1], token_terms[2]), "member")
    totalled = lax.psum(dominant_summands + trailing_summands, ("member", "node"))
    large_sums = totalled[:3]
    small_sums = totalled[3:]
    return (
        vertex_sensitivity[None],
        large_sums[0],
        large_sums[1],
        small_sums[0],
        small_sums[1],
        small_sums[2],
        piece_totals[0],
        piece_totals[1],
        piece_totals[2],
        large_sums[2],
    )


def solution(mesh):
    placed = (
        P("member", "node", None),
        P("member", "node", None),
        P(),
        P(),
        P(),
        P(),
        P(),
        P(),
        P(),
        P(),
        P(),
    )
    return jax.shard_map(
        shards,
        mesh=mesh,
        in_specs=placed,
        out_specs=(P("member", "node", None), P(), P(), P(), P(), P(), P(), P(), P(), P()),
        check_vma=False,
    )
```

profile of v0, /device:TPU:0, one launch (start us, length us, event | category | flops | bytes accessed | tf_op | source)
XLA Modules:
  0.0 231.0 jit_solution(12777113176723076068)
XLA Ops:
  7.3 1.1 copy-done
  8.4 1.2 convolution_convert_fusion.3
  9.7 0.5 fusion.6
  10.2 0.4 convolution_convert_fusion.2
  10.7 1.1 exponential_reduce_fusion
  11.8 1.0 fusion.31
  12.8 0.9 copy-done.10
  13.8 0.7 fusion.37
  14.4 0.7 fusion.35
  15.1 64.9 %all-reduce.2 = (f32[8,32,16]{1,2,0:T(8,128)}, f32[8,32]{1,0:T(8,128)S(1)}, f32[8,32,16]{1,2,0:T(8,128)S(1)}) all-reduce(f32[8,32,16]{1,2,0:T(8,128)S(1)} %fusion.35, f32[8,32]{1,0:T(8,128)S(1)} %get-tuple-element.32, f32[8,32,16]{1,2,0:T(8,128)S(1)} %fusion.37), channel_id=1, replica_groups=mesh['member'=2,'node'=16] {'node'}, use_global_device_ids=true, to_apply=%region_1.0 | all-reduce | flops 8448 | bytes 67584 | tf_op jit(solution)/shard_map/psum | solution.py:77
  80.0 1.1 fusion.22
  81.1 1.1 fusion.19
  82.2 1.1 fusion.25
  86.0 0.7 fusion.36
  87.3 1.1 fusion.9
  88.3 0.5 fusion.33
  88.8 1.0 copy-done.3
  89.8 1.1 convolution_bitcast_fusion.1
  90.9 0.7 fusion.4
  91.6 1.4 copy-done.11
  93.1 1.9 multiply_reduce_fusion
  95.0 1.3 copy-done.7
  96.7 1.1 convolution_bitcast_fusion.2
  98.2 2.3 convolution_bitcast_fusion.6
  100.5 1.8 fusion.38
  102.4 3.4 %fusion.5 = f32[1,4096,128]{2,1,0:T(8,128)} fusion(f32[4096,128]{1,0:T(8,128)} %fusion.38, bf16[4096,128]{0,1:T(8,128)(2,1)S(1)} %bitcast.108, bf16[128,128]{1,0:T(8,128)(2,1)S(1)} %copy-done.15), kind=kOutput, calls=%fused_computation.7 | convolution fusion | flops 134742016 | bytes 5275648 | tf_op jit(solution)/shard_map/dot_general | solution.py:153
  105.8 37.0 %all-reduce = (f32[128]{0:T(128)}, f32[16,32]{1,0:T(8,128)}, f32[8]{0:T(128)}) all-reduce(f32[128]{0:T(128)S(1)} %reduce_sum.85, f32[16,32]{1,0:T(8,128)S(1)} %convolution_bitcast_fusion.6, f32[8]{0:T(128)S(1)} %negate_divide_fusion), channel_id=1, replica_groups=mesh['member'=2,'node'=16] {'member','node'}, use_global_device_ids=true, to_apply=%region_12.0 | all-reduce | flops 648 | bytes 5184 | tf_op jit(solution)/shard_map/psum | solution.py:158
  143.0 9.7 %all-reduce.3 = (f32[16,16]{1,0:T(8,128)}, f32[16,16]{1,0:T(8,128)}, f32[16,16]{1,0:T(8,128)}) all-reduce(f32[16,16]{1,0:T(8,128)S(1)} %convolution_bitcast_fusion.5, f32[16,16]{1,0:T(8,128)S(1)} %convolution_bitcast_fusion.4, f32[16,16]{1,0:T(8,128)S(1)} %convolution_bitcast_fusion.3), channel_id=1, replica_groups=mesh['member'=2,'node'=16] {'member'}, use_global_device_ids=true, to_apply=%region_16.0 | all-reduce | flops 768 | bytes 6144 | tf_op jit(solution)/shard_map/psum | solution.py:157
  152.7 66.8 %all-reduce.6.cloned.1.call-done = (f32[128,128]{0,1:T(8,128)}, f32[128,128]{0,1:T(8,128)}, f32[128,128]{1,0:T(8,128)}) async-done(((f32[128,128]{0,1:T(8,128)}, f32[128,128]{0,1:T(8,128)}, f32[128,128]{1,0:T(8,128)}), (f32[128,128]{0,1:T(8,128)}, f32[128,128]{0,1:T(8,128)}, f32[128,128]{1,0:T(8,128)})) %all-reduce.6.cloned.1.call-update) | async-done | bytes 196624 | tf_op jit(solution)/shard_map/psum | solution.py:158
  219.5 1.6 copy.28
  221.1 1.6 copy.29
  222.7 1.5 copy.43
  (69 shorter events, 4.4 us)
Async XLA Ops:
  7.2 1.2 copy-start
  7.2 2.5 %copy-start.15 = (bf16[128,128]{1,0:T(8,128)(2,1)S(1)}, bf16[128,128]{1,0:T(8,128)(2,1)}, u32[]{:S(2)}) copy-start(bf16[128,128]{1,0:T(8,128)(2,1)} %param.14) | copy-start | bytes 98308
  7.2 2.5 %copy-start.24 = (f32[128]{0:T(128)S(1)}, f32[128]{0:T(128)}, u32[]{:S(2)}) copy-start(f32[128]{0:T(128)} %param.15) | copy-start | bytes 1540
  7.2 3.0 %copy-start.12 = (bf16[1,4096,128]{2,1,0:T(8,128)(2,1)S(1)}, bf16[1,4096,128]{2,1,0:T(8,128)(2,1)}, u32[]{:S(2)}) copy-start(bf16[1,4096,128]{2,1,0:T(8,128)(2,1)} %param.12) | copy-start | bytes 3145732
  7.2 3.0 %copy-start.19 = (bf16[128,128]{1,0:T(8,128)(2,1)S(1)}, bf16[128,128]{1,0:T(8,128)(2,1)}, u32[]{:S(2)}) copy-start(bf16[128,128]{1,0:T(8,128)(2,1)} %param.21) | copy-start | bytes 98308
  7.2 212.3 %all-reduce.6.cloned.1.call-start = ((), (), s32[]{:S(2)}) async-start(), calls=%async_computation | async-start | bytes 393216 | tf_op jit(solution)/shard_map/psum | solution.py:158
  9.7 1.0 copy-start.8
  9.7 1.0 copy-start.21
  9.7 1.0 copy-start.25
  10.2 4.2 %copy-start.5 = (bf16[4096,128]{0,1:T(8,128)(2,1)}, bf16[4096,128]{0,1:T(8,128)(2,1)S(1)}, u32[]{:S(2)}) copy-start(bf16[4096,128]{0,1:T(8,128)(2,1)S(1)} %fusion.6) | copy-start | bytes 3145732
  10.7 3.1 %copy-start.1 = (bf16[4096,128]{0,1:T(8,128)(2,1)}, bf16[4096,128]{0,1:T(8,128)(2,1)S(1)}, u32[]{:S(2)}) copy-start(bf16[4096,128]{0,1:T(8,128)(2,1)S(1)} %convolution_convert_fusion.2) | copy-start | bytes 3145732
  11.8 1.9 copy-start.10
  14.4 65.6 %copy-start.23 = (bf16[16,16]{1,0:T(8,128)(2,1)S(1)}, bf16[16,16]{1,0:T(8,128)(2,1)}, u32[]{:S(2)}) copy-start(bf16[16,16]{1,0:T(8,128)(2,1)} %param.19) | copy-start | bytes 1540
  14.4 66.7 %copy-start.22 = (bf16[16,16]{1,0:T(8,128)(2,1)S(1)}, bf16[16,16]{1,0:T(8,128)(2,1)}, u32[]{:S(2)}) copy-start(bf16[16,16]{1,0:T(8,128)(2,1)} %param.20) | copy-start | bytes 1540
  14.4 67.8 %copy-start.20 = (bf16[16,16]{1,0:T(8,128)(2,1)S(1)}, bf16[16,16]{1,0:T(8,128)(2,1)}, u32[]{:S(2)}) copy-start(bf16[16,16]{1,0:T(8,128)(2,1)} %param.18) | copy-start | bytes 1540
  84.3 2.4 %copy-start.16 = (f32[8,32,16]{1,2,0:T(8,128)}, f32[8,32,16]{1,2,0:T(8,128)S(1)}, u32[]{:S(2)}) copy-start(f32[8,32,16]{1,2,0:T(8,128)S(1)} %fusion.16) | copy-start | bytes 49156
  84.8 1.2 copy-start.2
  86.0 1.1 copy-start.18
  86.0 1.3 copy-start.13
  88.3 2.6 %copy-start.6 = (bf16[4096,128]{0,1:T(8,128)(2,1)S(1)}, bf16[4096,128]{0,1:T(8,128)(2,1)}, u32[]{:S(2)}) copy-start(bf16[4096,128]{0,1:T(8,128)(2,1)} %copy-done.5) | copy-start | bytes 3145732
  88.8 1.0 copy-start.3
  90.9 2.2 copy-start.11
  94.9 1.3 copy-start.7
  96.7 1.5 copy-start.9
  97.8 2.7 %copy-start.14 = (bf16[128,128]{1,0:T(8,128)(2,1)S(1)}, bf16[128,128]{1,0:T(8,128)(2,1)}, u32[]{:S(2)}) copy-start(bf16[128,128]{1,0:T(8,128)(2,1)} %param.13) | copy-start | bytes 98308
  100.5 1.9 copy-start.4
  102.4 40.5 %copy-start.17 = (f32[8,32,16]{1,2,0:T(8,128)S(1)}, f32[8,32,16]{1,2,0:T(8,128)}, u32[]{:S(2)}) copy-start(f32[8,32,16]{1,2,0:T(8,128)} %copy-done.16) | copy-start | bytes 49156
Sparse Core Ops, SparseCore 0:
  97.9 121.5 all-reduce.5
where the time goes:
time: 232 us; the launch traced here: 231 us
  blocking collectives  112 us (48%)
  waiting for transfers between devices  66.8 us (29%)
  matrix products  24.3 us (10%)
  between operations  14.5 us (6%)
  local copies, waits for them, and re-layouts  10.8 us (5%)
  other arithmetic  2.87 us (1%)
    psum x1, waiting for transfers between devices, shards(): lax.psum(dominant_summands + trailing_summands, ('member', 'node'))  66.8 us
    psum x1, blocking collectives, shards(): lax.psum((pooled_numerator, denominator), 'node')  64.9 us
    psum x1, blocking collectives, shards(): lax.psum(dominant_summands + trailing_summands, ('member', 'node'))  37 us
    unnamed x55, local copies, waits for them, and re-layouts  10.7 us
    psum x1, blocking collectives, shards(): lax.psum((token_terms[0], token_terms[1], token_terms[2]), 'member')  9.71 us
  transfers between devices with their start and end apart: 1, of which 1 were waited for; matrix products, arithmetic and copies ran while one was open for 4% of the time, Pallas kernels for 0%

commit v1 on v0

v1 whole, which is shorter than its diff:
```python
import functools
import math

import jax
import jax.numpy as jnp
from jax import lax
from jax.experimental import pallas as pl
from jax.experimental.pallas import tpu as pltpu
from jax.sharding import PartitionSpec as P

W = 128
HEADS = 8
M = 32
D = 16
S = HEADS * M
LOW = 4
CHUNK = 512
EPS = 1e-05
F32 = jnp.float32
BF16 = jnp.bfloat16
HIGHEST = lax.Precision.HIGHEST
MESH = pl.DeviceIdType.MESH

NN = (((1,), (0,)), ((), ()))
NT = (((1,), (1,)), ((), ()))
TN = (((0,), (0,)), ((), ()))


def dot(a, b, dims=NN):
    return lax.dot_general(a, b, dims, preferred_element_type=F32)


def dot32(a, b, dims=NN):
    return lax.dot_general(a, b, dims, precision=HIGHEST, preferred_element_type=F32)


def iota(shape, axis):
    return lax.broadcasted_iota(jnp.int32, shape, axis)


def group_sum(values, ones):
    upper = values.astype(BF16)
    lower = (values - upper.astype(F32)).astype(BF16)
    return dot(upper, ones) + dot(lower, ones)


def fold_rows(a, step):
    total = a[0:step]
    for i in range(step, a.shape[0], step):
        total = total + a[i : i + step]
    return total


def main_kernel(
    n_member, n_node, parts, part_rows,
    s_ref, x_hbm, g_hbm, w1_ref, w2_ref, off_ref, a_ref, wq_ref, wk_ref, wv_ref, w3_ref,
    packed_ref, mf_hbm,
    x_ref, g_ref, mid_ref, fb_ref, pb_ref, probs_ref, logits_ref, mf_ref,
    pool_acc, den_acc, xg_acc, slice_acc, proj_acc, bias_acc, temp_acc,
    pool_src, pool_recv, pool_z, pool_full, grad_src, grad_recv, grad_z, grad_full,
    in_sem, out_sem,
    a_send, a_recv, b_send, b_recv, c_send, c_recv,
    d_send, d_recv, e_send, e_recv, f_send, f_recv,
):
    rows = x_ref.shape[0]
    high_n = n_node // LOW
    member, node = lax.axis_index("member"), lax.axis_index("node")
    low, high = lax.rem(node, LOW), lax.div(node, LOW)
    group = member * LOW + low

    def low_peer(k):
        return lax.rem(low + k, LOW)

    def high_peer(k):
        return lax.rem(high + k, high_n)

    def group_peer(k):
        return lax.rem(group + k, parts)

    def low_id(k):
        return (member, high * LOW + low_peer(k))

    def high_id(k):
        return (member, high_peer(k) * LOW + low)

    def group_id(k):
        peer = group_peer(k)
        return (lax.div(peer, LOW), high * LOW + lax.rem(peer, LOW))

    load_x = pltpu.make_async_copy(x_hbm, x_ref, in_sem.at[0])
    load_g = pltpu.make_async_copy(g_hbm, g_ref, in_sem.at[1])
    load_x.start()
    load_g.start()

    barrier = pltpu.get_barrier_semaphore()
    for k in range(1, parts):
        pl.semaphore_signal(barrier, inc=1, device_id=group_id(k), device_id_type=MESH)
    for k in range(1, high_n):
        pl.semaphore_signal(barrier, inc=1, device_id=high_id(k), device_id_type=MESH)

    def send(src, dst, send_sem, recv_sem, target):
        copy = pltpu.make_async_remote_copy(
            src_ref=src, dst_ref=dst, send_sem=send_sem, recv_sem=recv_sem,
            device_id=target, device_id_type=MESH,
        )
        copy.start()
        return copy

    head_of_slice = iota((1, S), 1) // M
    inv_s = jnp.zeros((1, S), F32)
    for h in range(HEADS):
        inv_s = jnp.where(head_of_slice == h, 1.0 / jnp.full((1, S), s_ref[h], F32), inv_s)
    ones = jnp.where(iota((S, S), 0) // M == iota((S, S), 1) // M, 1.0, 0.0).astype(BF16)
    same_head = iota((W, S), 0) // D == iota((W, S), 1) // M
    pick_rows = jnp.where(iota((W, D), 0) % D == iota((W, D), 1), 1.0, 0.0).astype(BF16)
    pick_slices = jnp.where(iota((M, S), 1) % M == iota((M, S), 0), 1.0, 0.0).astype(BF16)
    pick_columns = jnp.where(iota((D, W), 1) % D == iota((D, W), 0), 1.0, 0.0).astype(BF16)
    a_all = dot(dot(pick_rows, a_ref[...]).astype(BF16), pick_slices)
    a_block = jnp.where(same_head, a_all, 0.0).astype(BF16)
    head_square = iota((W, W), 0) // D == iota((W, W), 1) // D

    def square_block(ref):
        return jnp.where(
            head_square, dot(dot(pick_rows, ref[...]).astype(BF16), pick_columns), 0.0
        )

    w12 = jnp.concatenate([w1_ref[...], w2_ref[...]], axis=1)
    w3 = w3_ref[...]
    offset = off_ref[...]

    pool_acc[...] = jnp.zeros_like(pool_acc)
    den_acc[...] = jnp.zeros_like(den_acc)
    load_x.wait()
    load_g.wait()

    def first(i, carry):
        at = pl.ds(pl.multiple_of(i * CHUNK, CHUNK), CHUNK)
        x = x_ref[at, :]
        both = dot(x, w12)
        mid = both[:, :W].astype(BF16)
        feat = (both[:, W:] + offset).astype(BF16)
        back = dot(g_ref[at, :], w3, NT).astype(BF16)
        logits = dot(mid, a_block) * inv_s
        e = jnp.exp(logits)
        probs = e / group_sum(e, ones)
        pb = probs.astype(BF16)
        fb = jnp.concatenate([back, feat], axis=1)
        mid_ref[at, :] = mid
        fb_ref[at, :] = fb
        pb_ref[at, :] = pb
        probs_ref[at, :] = probs
        logits_ref[at, :] = logits
        pool_acc[...] += dot(pb, fb, TN)
        den_acc[...] += jnp.sum(probs.reshape(CHUNK // 8, 8, S), axis=0)
        return carry

    lax.fori_loop(0, rows // CHUNK, first, 0)

    slice_head = iota((S, W), 0) // M == iota((S, W), 1) // D
    token_grad = fold_rows(jnp.where(slice_head, pool_acc[:, :W], 0.0), M)
    numer = fold_rows(jnp.where(slice_head, pool_acc[:, W:], 0.0), M)
    den = jnp.sum(den_acc[...], axis=0, keepdims=True)
    for p in range(LOW):
        pool_src[p, 0:8, :] = numer[8 * p : 8 * p + 8]
        pool_src[p, 8:16, :] = token_grad[8 * p : 8 * p + 8]
        piece = den[:, (p % 2) * W : (p % 2 + 1) * W]
        pool_src[p, 16:24, :] = jnp.broadcast_to(piece, (8, W))

    pl.semaphore_wait(barrier, parts - 1 + high_n - 1)

    copies = [
        send(pool_src.at[low_peer(k)], pool_recv.at[k - 1], a_send.at[k - 1], a_recv.at[k - 1], low_id(k))
        for k in range(1, LOW)
    ]
    total = pool_src[low]
    for k, copy in enumerate(copies):
        copy.wait()
        total = total + pool_recv[k]
    pool_z[high] = total
    copies = [
        send(pool_z.at[high], pool_z.at[high], b_send.at[k - 1], b_recv.at[k - 1], high_id(k))
        for k in range(1, high_n)
    ]
    for copy in copies:
        copy.wait()
    total = pool_z[0]
    for k in range(1, high_n):
        total = total + pool_z[k]
    pool_full[low] = total
    copies = [
        send(pool_full.at[low], pool_full.at[low], c_send.at[k - 1], c_recv.at[k - 1], low_id(k))
        for k in range(1, LOW)
    ]
    for copy in copies:
        copy.wait()

    numer = jnp.concatenate([pool_full[p, 0:8, :] for p in range(LOW)], axis=0)
    token_grad = jnp.concatenate([pool_full[p, 8:16, :] for p in range(LOW)], axis=0)
    den = jnp.concatenate([pool_full[p, 16:17, :] for p in range(2)], axis=1)
    eye = iota((S, S), 0) == iota((S, S), 1)
    den = jnp.sum(jnp.where(eye, den, 0.0), axis=1, keepdims=True)
    inverse = 1.0 / (den + EPS)
    numer = jnp.where(slice_head, jnp.concatenate([numer] * HEADS, axis=0), 0.0)
    token_grad = jnp.where(slice_head, jnp.concatenate([token_grad] * HEADS, axis=0), 0.0)
    tokens = numer / (den + EPS)
    maps = jnp.concatenate([square_block(r) for r in (wq_ref, wk_ref, wv_ref)], axis=1)
    qkv = dot32(tokens, maps)
    q, k, v = qkv[:, :W], qkv[:, W : 2 * W], qkv[:, 2 * W :]
    inside = iota((S, S), 0) // M == iota((S, S), 1) // M
    scale = 1.0 / math.sqrt(D)
    scores = jnp.where(inside, dot32(q, k, NT) * scale, 0.0)
    e = jnp.where(inside, jnp.exp(scores), 0.0)
    share = e / jnp.sum(e, axis=1, keepdims=True)
    token_out = dot32(share, v).astype(BF16)
    d_share = dot32(token_grad, v, NT)
    d_scores = share * (d_share - jnp.sum(share * d_share, axis=1, keepdims=True)) * scale
    d_qkv = jnp.concatenate(
        [dot32(d_scores, k), dot32(d_scores, q, TN), dot32(share, token_grad, TN)], axis=1
    )
    tok_back = dot32(d_qkv, maps, NT)
    numer_back = (tok_back * inverse).astype(BF16)
    den_back = -jnp.sum(tok_back * tokens, axis=1, keepdims=True) * inverse
    den_back = jnp.sum(jnp.where(eye, den_back, 0.0), axis=0, keepdims=True)
    d_maps = dot32(tokens, d_qkv, TN)
    mix = jnp.concatenate([token_out, numer_back], axis=1)

    xg_acc[...] = jnp.zeros_like(xg_acc)
    slice_acc[...] = jnp.zeros_like(slice_acc)
    proj_acc[...] = jnp.zeros_like(proj_acc)
    bias_acc[...] = jnp.zeros_like(bias_acc)
    temp_acc[...] = jnp.zeros_like(temp_acc)

    def second(i, carry):
        at = pl.ds(pl.multiple_of(i * CHUNK, CHUNK), CHUNK)
        probs = probs_ref[at, :]
        both = dot(pb_ref[at, :], mix)
        mixed = both[:, :W].astype(BF16)
        feat_back = both[:, W:]
        bias_acc[...] += jnp.sum(feat_back.reshape(CHUNK // 8, 8, W), axis=0)
        proj_acc[...] += dot(mixed, g_ref[at, :], TN)
        prob_back = dot(fb_ref[at, :], mix, NT) + den_back
        inner = group_sum(probs * prob_back, ones)
        logit_back = probs * (prob_back - inner)
        temp_acc[...] += jnp.sum((logit_back * logits_ref[at, :]).reshape(CHUNK // 8, 8, S), axis=0)
        score_back = (logit_back * inv_s).astype(BF16)
        mid_back = dot(score_back, a_block, NT).astype(BF16)
        mf = jnp.concatenate([mid_back, feat_back.astype(BF16)], axis=1)
        mf_ref[at, :] = mf
        xg_acc[...] += dot(x_ref[at, :], mf, TN)
        slice_acc[...] += dot(mid_ref[at, :], score_back, TN)
        return carry

    lax.fori_loop(0, rows // CHUNK, second, 0)
    store_mf = pltpu.make_async_copy(mf_ref, mf_hbm, out_sem)
    store_mf.start()

    grad_src[0:W, :] = xg_acc[:, :W]
    grad_src[W : 2 * W, :] = xg_acc[:, W:]
    grad_src[2 * W : 3 * W, :] = proj_acc[...]
    slices = fold_rows(jnp.where(same_head, slice_acc[...], 0.0), D)
    slices = slices[:, :W] + slices[:, W:]
    slices = slices + pltpu.roll(slices, 64, 1)
    slices = slices + pltpu.roll(slices, 32, 1)
    lane = iota((D, W), 1)
    owner = (node == 0).astype(F32)
    block = jnp.where(lane < M, slices, 0.0)
    for i in range(3):
        term = fold_rows(d_maps[:, i * W : (i + 1) * W], D)
        for shift in (64, 32, 16):
            term = term + pltpu.roll(term, shift, 1)
        start = M + i * D
        block = jnp.where((lane >= start) & (lane < start + D), term * owner, block)
    grad_src[3 * W : 3 * W + D, :] = block
    pick_heads = jnp.where(iota((S, W), 0) // M == iota((S, W), 1), 1.0, 0.0)
    temp = jnp.sum(dot32(temp_acc[...] * -inv_s, pick_heads), axis=0, keepdims=True)
    bias = jnp.sum(bias_acc[...], axis=0, keepdims=True)
    row = iota((8, W), 0)
    grad_src[3 * W + D : 3 * W + D + 8, :] = jnp.where(row == 0, bias, jnp.where(row == 1, temp, 0.0))
    used = 3 * W + D + 8
    if used < parts * part_rows:
        grad_src[used:, :] = jnp.zeros((parts * part_rows - used, W), F32)

    def part(ref, p):
        return ref.at[pl.ds(pl.multiple_of(p * part_rows, 8), part_rows), :]

    copies = [
        send(part(grad_src, group_peer(k)), grad_recv.at[k - 1], d_send.at[k - 1], d_recv.at[k - 1], group_id(k))
        for k in range(1, parts)
    ]
    total = part(grad_src, group)[...]
    for k, copy in enumerate(copies):
        copy.wait()
        total = total + grad_recv[k]
    grad_z[high] = total
    copies = [
        send(grad_z.at[high], grad_z.at[high], e_send.at[k - 1], e_recv.at[k - 1], high_id(k))
        for k in range(1, high_n)
    ]
    for copy in copies:
        copy.wait()
    total = grad_z[0]
    for k in range(1, high_n):
        total = total + grad_z[k]
    mine = part(grad_full, group)
    mine[...] = total
    copies = [
        send(mine, mine, f_send.at[k - 1], f_recv.at[k - 1], group_id(k)) for k in range(1, parts)
    ]
    for copy in copies:
        copy.wait()
    packed_ref[...] = grad_full[...]
    store_mf.wait()


def final_kernel(
    packed_ref, mf_ref, w1_ref, w2_ref,
    out_ref, mid_ref, feature_ref, bias_ref, slice_ref, temp_ref, query_ref, key_ref, value_ref, proj_ref,
):
    w12 = jnp.concatenate([w1_ref[...], w2_ref[...]], axis=1)
    out_ref[...] = dot(mf_ref[...], w12, NT)

    @pl.when(pl.program_id(0) == 0)
    def _():
        mid_ref[...] = packed_ref[0:W, :]
        feature_ref[...] = packed_ref[W : 2 * W, :]
        proj_ref[...] = packed_ref[2 * W : 3 * W, :]
        block = packed_ref[3 * W : 3 * W + D, :]
        slice_ref[...] = block[:, 0:M]
        query_ref[...] = block[:, M : M + D]
        key_ref[...] = block[:, M + D : M + 2 * D]
        value_ref[...] = block[:, M + 2 * D : M + 3 * D]
        bias_ref[...] = packed_ref[3 * W + D : 3 * W + D + 1, :]
        temp_ref[...] = packed_ref[3 * W + D + 1 : 3 * W + D + 2, 0:HEADS]


def shards(n_member, n_node, x, g, w1, w2, offset, a, s, wq, wk, wv, w3):
    x, g = x[0], g[0]
    rows = x.shape[0]
    high_n = n_node // LOW
    parts = n_member * LOW
    used = 3 * W + D + 8
    part_rows = -(-used // (8 * parts)) * 8
    vmem = pl.BlockSpec(memory_space=pltpu.VMEM)
    hbm = pl.BlockSpec(memory_space=pl.ANY)
    dma = pltpu.SemaphoreType.DMA
    flops = 2 * rows * S * S * 12
    packed, mf = pl.pallas_call(
        functools.partial(main_kernel, n_member, n_node, parts, part_rows),
        out_shape=(
            jax.ShapeDtypeStruct((parts * part_rows, W), F32),
            jax.ShapeDtypeStruct((rows, 2 * W), BF16),
        ),
        in_specs=[pl.BlockSpec(memory_space=pltpu.SMEM), hbm, hbm] + [vmem] * 8,
        out_specs=(vmem, hbm),
        scratch_shapes=[
            pltpu.VMEM((rows, W), BF16),
            pltpu.VMEM((rows, W), BF16),
            pltpu.VMEM((rows, W), BF16),
            pltpu.VMEM((rows, 2 * W), BF16),
            pltpu.VMEM((rows, S), BF16),
            pltpu.VMEM((rows, S), F32),
            pltpu.VMEM((rows, S), F32),
            pltpu.VMEM((rows, 2 * W), BF16),
            pltpu.VMEM((S, 2 * W), F32),
            pltpu.VMEM((8, S), F32),
            pltpu.VMEM((W, 2 * W), F32),
            pltpu.VMEM((W, S), F32),
            pltpu.VMEM((W, W), F32),
            pltpu.VMEM((8, W), F32),
            pltpu.VMEM((8, S), F32),
            pltpu.VMEM((LOW, 24, W), F32),
            pltpu.VMEM((LOW - 1, 24, W), F32),
            pltpu.VMEM((high_n, 24, W), F32),
            pltpu.VMEM((LOW, 24, W), F32),
            pltpu.VMEM((parts * part_rows, W), F32),
            pltpu.VMEM((parts - 1, part_rows, W), F32),
            pltpu.VMEM((high_n, part_rows, W), F32),
            pltpu.VMEM((parts * part_rows, W), F32),
            dma((2,)),
            dma,
            dma((LOW - 1,)), dma((LOW - 1,)),
            dma((high_n - 1,)), dma((high_n - 1,)),
            dma((LOW - 1,)), dma((LOW - 1,)),
            dma((parts - 1,)), dma((parts - 1,)),
            dma((high_n - 1,)), dma((high_n - 1,)),
            dma((parts - 1,)), dma((parts - 1,)),
        ],
        compiler_params=pltpu.CompilerParams(
            collective_id=0, has_side_effects=True, vmem_limit_bytes=48 * 1024 * 1024
        ),
        cost_estimate=pl.CostEstimate(
            flops=flops, bytes_accessed=rows * W * 8, transcendentals=rows * S
        ),
        name="pool_and_gradients",
    )(s, x, g, w1, w2, offset.reshape(1, W), a, wq, wk, wv, w3)

    tile = 1024
    whole = lambda *shape: pl.BlockSpec(shape, lambda i: (0,) * len(shape))
    outs = pl.pallas_call(
        final_kernel,
        grid=(rows // tile,),
        out_shape=(
            jax.ShapeDtypeStruct((rows, W), F32),
            jax.ShapeDtypeStruct((W, W), F32),
            jax.ShapeDtypeStruct((W, W), F32),
            jax.ShapeDtypeStruct((1, W), F32),
            jax.ShapeDtypeStruct((D, M), F32),
            jax.ShapeDtypeStruct((1, HEADS), F32),
            jax.ShapeDtypeStruct((D, D), F32),
            jax.ShapeDtypeStruct((D, D), F32),
            jax.ShapeDtypeStruct((D, D), F32),
            jax.ShapeDtypeStruct((W, W), F32),
        ),
        in_specs=[
            whole(parts * part_rows, W),
            pl.BlockSpec((tile, 2 * W), lambda i: (i, 0)),
            whole(W, W),
            whole(W, W),
        ],
        out_specs=(
            pl.BlockSpec((tile, W), lambda i: (i, 0)),
            whole(W, W), whole(W, W), whole(1, W), whole(D, M), whole(1, HEADS),
            whole(D, D), whole(D, D), whole(D, D), whole(W, W),
        ),
        compiler_params=pltpu.CompilerParams(vmem_limit_bytes=32 * 1024 * 1024),
        cost_estimate=pl.CostEstimate(
            flops=2 * rows * 2 * W * W, bytes_accessed=rows * W * 8, transcendentals=0
        ),
        name="vertex_and_unpack",
    )(packed, mf, w1, w2)
    vertex, mid, feature, bias, slices, temp, query, key, value, proj = outs
    return (
        vertex[None], mid, feature, bias.reshape(W), slices, temp.reshape(HEADS),
        query, key, value, proj,
    )


def solution(mesh):
    spread = P("member", "node", None)
    return jax.shard_map(
        functools.partial(shards, mesh.shape["member"], mesh.shape["node"]),
        mesh=mesh,
        in_specs=(spread, spread) + (P(),) * 9,
        out_specs=(spread,) + (P(),) * 9,
        check_vma=False,
    )
```

time: 232 us -> 59.2 us (0.26)
  blocking collectives: 112 us -> 0 us
  waiting for transfers between devices: 66.8 us -> 0 us
  Pallas kernels: 0 us -> 49.3 us
  matrix products: 24.3 us -> 0 us
  between operations: 14.5 us -> 0.67 us
  other arithmetic: 2.87 us -> 0 us
    psum x3 -> x0, blocking collectives: 112 us -> none  [the longest x1 64.9 us: shards(): lax.psum((pooled_numerator, denominator), 'node')]
    psum x1 -> x0, waiting for transfers between devices: 66.8 us -> none  [shards(): lax.psum(dominant_summands + trailing_summands, ('member', 'node'))]
    pallas_call x0 -> x2, Pallas kernels: none -> 49.3 us  [the longest x1 46.6 us: shards(): pl.pallas_call(functools.partial(main_kernel, n_member, n_node, parts, pa...]
    dot_general x32 -> x0, matrix products: 24.3 us -> none  [the longest x1 3.41 us: shards(): jnp.dot(feat_back_half, aggregate_projection.T, preferred_element_type=jn...]
    unnamed x55 -> x22, local copies, waits for them, and re-layouts: 10.7 us -> 8.77 us
  transfers between devices with their start and end apart: 1 -> 0, of which waited for: 1 -> 0; matrix products, arithmetic and copies ran while one was open for 4% -> 0% of each run, Pallas kernels for 0% -> 0%
where the time goes in v1:
time: 59.2 us; the launch traced here: 58.7 us
  Pallas kernels  49.3 us (83%)
  local copies, waits for them, and re-layouts  8.77 us (15%)
  between operations  0.67 us (1%)
    pallas_call x1, Pallas kernels, shards(): pl.pallas_call(functools.partial(main_kernel, n_member, n_node, parts, pa...  46.6 us
    unnamed x22, local copies, waits for them, and re-layouts  8.77 us
    pallas_call x1, Pallas kernels, shards(): pl.pallas_call(final_kernel, grid=(rows // tile,), out_shape=(jax.ShapeDt...  2.65 us

profile of v1, /device:TPU:0, one launch (start us, length us, event | category | flops | bytes accessed | tf_op | source)
XLA Modules:
  0.0 58.7 jit_solution(14766655685521734314)
XLA Ops:
  0.6 0.0 copy-start
  0.7 0.7 %copy-done = bf16[128,128]{1,0:T(8,128)(2,1)S(1)} copy-done((bf16[128,128]{1,0:T(8,128)(2,1)S(1)}, bf16[128,128]{1,0:T(8,128)(2,1)}, u32[]{:S(2)}) %copy-start) | copy-done | bytes 32792
  1.4 0.0 copy-start.1
  1.4 0.8 %copy-done.1 = bf16[128,128]{1,0:T(8,128)(2,1)S(1)} copy-done((bf16[128,128]{1,0:T(8,128)(2,1)S(1)}, bf16[128,128]{1,0:T(8,128)(2,1)}, u32[]{:S(2)}) %copy-start.1) | copy-done | bytes 32792
  2.2 0.0 copy-start.2
  2.2 1.2 %copy-done.2 = bf16[1,4096,128]{2,1,0:T(8,128)(2,1)S(1)} copy-done((bf16[1,4096,128]{2,1,0:T(8,128)(2,1)S(1)}, bf16[1,4096,128]{2,1,0:T(8,128)(2,1)}, u32[]{:S(2)}) %copy-start.2) | copy-done | bytes 1048600
  3.4 0.0 copy-start.3
  3.4 1.2 %copy-done.3 = bf16[1,4096,128]{2,1,0:T(8,128)(2,1)S(1)} copy-done((bf16[1,4096,128]{2,1,0:T(8,128)(2,1)S(1)}, bf16[1,4096,128]{2,1,0:T(8,128)(2,1)}, u32[]{:S(2)}) %copy-start.3) | copy-done | bytes 1048600
  4.6 0.0 copy-start.4
  4.6 0.8 %copy-done.4 = bf16[128,128]{1,0:T(8,128)(2,1)S(1)} copy-done((bf16[128,128]{1,0:T(8,128)(2,1)S(1)}, bf16[128,128]{1,0:T(8,128)(2,1)}, u32[]{:S(2)}) %copy-start.4) | copy-done | bytes 32792
  5.4 0.0 copy-start.5
  5.4 0.7 %copy-done.5 = bf16[16,32]{1,0:T(8,128)(2,1)S(1)} copy-done((bf16[16,32]{1,0:T(8,128)(2,1)S(1)}, bf16[16,32]{1,0:T(8,128)(2,1)}, u32[]{:S(2)}) %copy-start.5) | copy-done | bytes 1048
  6.1 0.0 copy-start.6
  6.1 0.7 %copy-done.6 = bf16[16,16]{1,0:T(8,128)(2,1)S(1)} copy-done((bf16[16,16]{1,0:T(8,128)(2,1)S(1)}, bf16[16,16]{1,0:T(8,128)(2,1)}, u32[]{:S(2)}) %copy-start.6) | copy-done | bytes 536
  6.7 0.0 copy-start.7
  6.8 0.7 %copy-done.7 = bf16[16,16]{1,0:T(8,128)(2,1)S(1)} copy-done((bf16[16,16]{1,0:T(8,128)(2,1)S(1)}, bf16[16,16]{1,0:T(8,128)(2,1)}, u32[]{:S(2)}) %copy-start.7) | copy-done | bytes 536
  7.4 0.0 copy-start.8
  7.4 0.7 %copy-done.8 = bf16[16,16]{1,0:T(8,128)(2,1)S(1)} copy-done((bf16[16,16]{1,0:T(8,128)(2,1)S(1)}, bf16[16,16]{1,0:T(8,128)(2,1)}, u32[]{:S(2)}) %copy-start.8) | copy-done | bytes 536
  8.1 0.0 copy-start.9
  8.1 0.7 %copy-done.9 = f32[8]{0:T(128)S(1)} copy-done((f32[8]{0:T(128)S(1)}, f32[8]{0:T(128)}, u32[]{:S(2)}) %copy-start.9) | copy-done | bytes 56
  8.8 0.0 copy-start.10
  8.8 0.7 %copy-done.10 = f32[128]{0:T(128)S(1)} copy-done((f32[128]{0:T(128)S(1)}, f32[128]{0:T(128)}, u32[]{:S(2)}) %copy-start.10) | copy-done | bytes 536
  9.4 46.6 %pool_and_gradients.1 = (f32[448,128]{1,0:T(8,128)S(1)}, bf16[4096,256]{1,0:T(8,128)(2,1)S(1)}) custom-call(f32[8]{0:T(128)S(1)} %copy-done.9, bf16[4096,128]{1,0:T(8,128)(2,1)S(1)} %bitcast.6, bf16[4096,128]{1,0:T(8,128)(2,1)S(1)} %bitcast.7, bf16[128,128]{1,0:T(8,128)(2,1)S(1)} %copy-done, bf16[128,128]{1,0:T(8,128)(2,1)S(1)} %copy-done.1, ...), custom_call_target="tpu_custom_call" | custom-call | flops 6442450944 | bytes 4194304 | tf_op jit(solution)/shard_map/pool_and_gradients/pallas_call | solution.py:347
  56.0 2.6 %vertex_and_unpack.1 = (f32[4096,128]{1,0:T(8,128)}, f32[128,128]{1,0:T(8,128)}, f32[128,128]{1,0:T(8,128)}, f32[1,128]{1,0:T(1,128)}, f32[16,32]{1,0:T(8,128)},...) custom-call(f32[448,128]{1,0:T(8,128)S(1)} %get-tuple-element.22.packed_ref, ...), custom_call_target="tpu_custom_call" | custom-call | flops 268435456 | bytes 4194304 | tf_op jit(solution)/shard_map/vertex_and_unpack/pallas_call | solution.py:399
Async XLA Ops:
  0.6 0.8 %copy-start = (bf16[128,128]{1,0:T(8,128)(2,1)S(1)}, bf16[128,128]{1,0:T(8,128)(2,1)}, u32[]{:S(2)}) copy-start(bf16[128,128]{1,0:T(8,128)(2,1)} %w1_ref.3) | copy-start | bytes 98308
  1.4 0.8 %copy-start.1 = (bf16[128,128]{1,0:T(8,128)(2,1)S(1)}, bf16[128,128]{1,0:T(8,128)(2,1)}, u32[]{:S(2)}) copy-start(bf16[128,128]{1,0:T(8,128)(2,1)} %w2_ref.3) | copy-start | bytes 98308
  2.2 1.2 %copy-start.2 = (bf16[1,4096,128]{2,1,0:T(8,128)(2,1)S(1)}, bf16[1,4096,128]{2,1,0:T(8,128)(2,1)}, u32[]{:S(2)}) copy-start(bf16[1,4096,128]{2,1,0:T(8,128)(2,1)} %param.11) | copy-start | bytes 3145732
  3.4 1.2 %copy-start.3 = (bf16[1,4096,128]{2,1,0:T(8,128)(2,1)S(1)}, bf16[1,4096,128]{2,1,0:T(8,128)(2,1)}, u32[]{:S(2)}) copy-start(bf16[1,4096,128]{2,1,0:T(8,128)(2,1)} %param.12) | copy-start | bytes 3145732
  4.6 0.8 %copy-start.4 = (bf16[128,128]{1,0:T(8,128)(2,1)S(1)}, bf16[128,128]{1,0:T(8,128)(2,1)}, u32[]{:S(2)}) copy-start(bf16[128,128]{1,0:T(8,128)(2,1)} %w3_ref.1) | copy-start | bytes 98308
  5.4 0.7 %copy-start.5 = (bf16[16,32]{1,0:T(8,128)(2,1)S(1)}, bf16[16,32]{1,0:T(8,128)(2,1)}, u32[]{:S(2)}) copy-start(bf16[16,32]{1,0:T(8,128)(2,1)} %a_ref.1) | copy-start | bytes 3076
  6.1 0.7 %copy-start.6 = (bf16[16,16]{1,0:T(8,128)(2,1)S(1)}, bf16[16,16]{1,0:T(8,128)(2,1)}, u32[]{:S(2)}) copy-start(bf16[16,16]{1,0:T(8,128)(2,1)} %wq_ref.1) | copy-start | bytes 1540
  6.7 0.7 %copy-start.7 = (bf16[16,16]{1,0:T(8,128)(2,1)S(1)}, bf16[16,16]{1,0:T(8,128)(2,1)}, u32[]{:S(2)}) copy-start(bf16[16,16]{1,0:T(8,128)(2,1)} %wk_ref.1) | copy-start | bytes 1540
  7.4 0.7 %copy-start.8 = (bf16[16,16]{1,0:T(8,128)(2,1)S(1)}, bf16[16,16]{1,0:T(8,128)(2,1)}, u32[]{:S(2)}) copy-start(bf16[16,16]{1,0:T(8,128)(2,1)} %wv_ref.1) | copy-start | bytes 1540
  8.1 0.7 %copy-start.9 = (f32[8]{0:T(128)S(1)}, f32[8]{0:T(128)}, u32[]{:S(2)}) copy-start(f32[8]{0:T(128)} %s_ref.1) | copy-start | bytes 100
  8.8 0.7 %copy-start.10 = (f32[128]{0:T(128)S(1)}, f32[128]{0:T(128)}, u32[]{:S(2)}) copy-start(f32[128]{0:T(128)} %param.15) | copy-start | bytes 1540

commit v2 on v1

--- a/solution.py
+++ b/solution.py
@@ -16,9 +16,9 @@
 LOW = 4
 CHUNK = 512
 EPS = 1e-05
+VMEM_LIMIT = 62 * 1024 * 1024
 F32 = jnp.float32
 BF16 = jnp.bfloat16
-HIGHEST = lax.Precision.HIGHEST
 MESH = pl.DeviceIdType.MESH
 
 NN = (((1,), (0,)), ((), ()))
@@ -30,8 +30,20 @@
     return lax.dot_general(a, b, dims, preferred_element_type=F32)
 
 
+def split(a):
+    upper = a.astype(BF16)
+    return upper, (a - upper.astype(F32)).astype(BF16)
+
+
 def dot32(a, b, dims=NN):
-    return lax.dot_general(a, b, dims, precision=HIGHEST, preferred_element_type=F32)
+    a_parts = (a,) if a.dtype == BF16 else split(a)
+    b_parts = (b,) if b.dtype == BF16 else split(b)
+    total = dot(a_parts[0], b_parts[0], dims)
+    if len(b_parts) == 2:
+        total = total + dot(a_parts[0], b_parts[1], dims)
+    if len(a_parts) == 2:
+        total = total + dot(a_parts[1], b_parts[0], dims)
+    return total
 
 
 def iota(shape, axis):
@@ -39,9 +51,7 @@
 
 
 def group_sum(values, ones):
-    upper = values.astype(BF16)
-    lower = (values - upper.astype(F32)).astype(BF16)
-    return dot(upper, ones) + dot(lower, ones)
+    return dot32(values, ones)
 
 
 def fold_rows(a, step):
@@ -52,15 +62,17 @@
 
 
 def main_kernel(
-    n_member, n_node, parts, part_rows,
+    n_member, n_node, parts, early_rows, late_rows,
     s_ref, x_hbm, g_hbm, w1_ref, w2_ref, off_ref, a_ref, wq_ref, wk_ref, wv_ref, w3_ref,
     packed_ref, mf_hbm,
     x_ref, g_ref, mid_ref, fb_ref, pb_ref, probs_ref, logits_ref, mf_ref,
-    pool_acc, den_acc, xg_acc, slice_acc, proj_acc, bias_acc, temp_acc,
-    pool_src, pool_recv, pool_z, pool_full, grad_src, grad_recv, grad_z, grad_full,
+    xt_ref, gt_ref, midt_ref,
+    pool_acc, den_acc, mid_acc, feature_acc, slice_acc, proj_acc, bias_acc, temp_acc,
+    pool_src, pool_recv, pool_z, pool_full,
+    early_src, early_recv, early_z, early_full, late_src, late_recv, late_z, late_full,
     in_sem, out_sem,
     a_send, a_recv, b_send, b_recv, c_send, c_recv,
-    d_send, d_recv, e_send, e_recv, f_send, f_recv,
+    early_sems, late_sems,
 ):
     rows = x_ref.shape[0]
     high_n = n_node // LOW
@@ -122,7 +134,7 @@
     def square_block(ref):
         return jnp.where(
             head_square, dot(dot(pick_rows, ref[...]).astype(BF16), pick_columns), 0.0
-        )
+        ).astype(BF16)
 
     w12 = jnp.concatenate([w1_ref[...], w2_ref[...]], axis=1)
     w3 = w3_ref[...]
@@ -172,6 +184,15 @@
         send(pool_src.at[low_peer(k)], pool_recv.at[k - 1], a_send.at[k - 1], a_recv.at[k - 1], low_id(k))
         for k in range(1, LOW)
     ]
+    def turn(source, target):
+        def step(i, carry):
+            at = pl.ds(pl.multiple_of(i * CHUNK, CHUNK), CHUNK)
+            target[i] = source[at, :].T
+            return carry
+
+        lax.fori_loop(0, rows // CHUNK, step, 0)
+
+    turn(x_ref, xt_ref)
     total = pool_src[low]
     for k, copy in enumerate(copies):
         copy.wait()
@@ -181,6 +202,8 @@
         send(pool_z.at[high], pool_z.at[high], b_send.at[k - 1], b_recv.at[k - 1], high_id(k))
         for k in range(1, high_n)
     ]
+    turn(g_ref, gt_ref)
+    turn(mid_ref, midt_ref)
     for copy in copies:
         copy.wait()
     total = pool_z[0]
@@ -224,39 +247,81 @@
     d_maps = dot32(tokens, d_qkv, TN)
     mix = jnp.concatenate([token_out, numer_back], axis=1)
 
-    xg_acc[...] = jnp.zeros_like(xg_acc)
-    slice_acc[...] = jnp.zeros_like(slice_acc)
-    proj_acc[...] = jnp.zeros_like(proj_acc)
-    bias_acc[...] = jnp.zeros_like(bias_acc)
-    temp_acc[...] = jnp.zeros_like(temp_acc)
+    for acc in (mid_acc, feature_acc, slice_acc, proj_acc, bias_acc, temp_acc):
+        acc[...] = jnp.zeros_like(acc)
+
+    def part(ref, p, size):
+        return ref.at[pl.ds(pl.multiple_of(p * size, 8), size), :]
+
+    def start_scatter(src, recv, size, sems):
+        return [
+            send(part(src, group_peer(k), size), recv.at[k - 1], sems.at[0, k - 1], sems.at[1, k - 1], group_id(k))
+            for k in range(1, parts)
+        ]
+
+    def start_across(copies, src, recv, z, size, sems):
+        total = part(src, group, size)[...]
+        for k, copy in enumerate(copies):
+            copy.wait()
+            total = total + recv[k]
+        z[high] = total
+        return [
+            send(z.at[high], z.at[high], sems.at[2, k - 1], sems.at[3, k - 1], high_id(k))
+            for k in range(1, high_n)
+        ]
+
+    def start_gather(copies, z, full, size, sems):
+        for copy in copies:
+            copy.wait()
+        total = z[0]
+        for k in range(1, high_n):
+            total = total + z[k]
+        mine = part(full, group, size)
+        mine[...] = total
+        return [
+            send(mine, mine, sems.at[4, k - 1], sems.at[5, k - 1], group_id(k))
+            for k in range(1, parts)
+        ]
 
     def second(i, carry):
         at = pl.ds(pl.multiple_of(i * CHUNK, CHUNK), CHUNK)
-        probs = probs_ref[at, :]
         both = dot(pb_ref[at, :], mix)
         mixed = both[:, :W].astype(BF16)
         feat_back = both[:, W:]
+        rounded = feat_back.astype(BF16)
+        mf_ref[at, W:] = rounded
         bias_acc[...] += jnp.sum(feat_back.reshape(CHUNK // 8, 8, W), axis=0)
-        proj_acc[...] += dot(mixed, g_ref[at, :], TN)
+        proj_acc[...] += dot(gt_ref[i], mixed)
+        feature_acc[...] += dot(xt_ref[i], rounded)
+        return carry
+
+    def third(i, carry):
+        at = pl.ds(pl.multiple_of(i * CHUNK, CHUNK), CHUNK)
+        probs = probs_ref[at, :]
         prob_back = dot(fb_ref[at, :], mix, NT) + den_back
         inner = group_sum(probs * prob_back, ones)
         logit_back = probs * (prob_back - inner)
         temp_acc[...] += jnp.sum((logit_back * logits_ref[at, :]).reshape(CHUNK // 8, 8, S), axis=0)
         score_back = (logit_back * inv_s).astype(BF16)
         mid_back = dot(score_back, a_block, NT).astype(BF16)
-        mf = jnp.concatenate([mid_back, feat_back.astype(BF16)], axis=1)
-        mf_ref[at, :] = mf
-        xg_acc[...] += dot(x_ref[at, :], mf, TN)
-        slice_acc[...] += dot(mid_ref[at, :], score_back, TN)
+        mf_ref[at, :W] = mid_back
+        mid_acc[...] += dot(xt_ref[i], mid_back)
+        slice_acc[...] += dot(midt_ref[i], score_back)
         return carry
 
-    lax.fori_loop(0, rows // CHUNK, second, 0)
+    steps = rows // CHUNK
+    lax.fori_loop(0, steps, second, 0)
+    early_src[0:W, :] = feature_acc[...]
+    early_src[W : 2 * W, :] = proj_acc[...].T
+    early = start_scatter(early_src, early_recv, early_rows, early_sems)
+    lax.fori_loop(0, steps // 2, third, 0)
+    early = start_across(early, early_src, early_recv, early_z, early_rows, early_sems)
+    lax.fori_loop(steps // 2, steps, third, 0)
     store_mf = pltpu.make_async_copy(mf_ref, mf_hbm, out_sem)
     store_mf.start()
-
-    grad_src[0:W, :] = xg_acc[:, :W]
-    grad_src[W : 2 * W, :] = xg_acc[:, W:]
-    grad_src[2 * W : 3 * W, :] = proj_acc[...]
+    early = start_gather(early, early_z, early_full, early_rows, early_sems)
+
+    late_src[0:W, :] = mid_acc[...]
     slices = fold_rows(jnp.where(same_head, slice_acc[...], 0.0), D)
     slices = slices[:, :W] + slices[:, W:]
     slices = slices + pltpu.roll(slices, 64, 1)
@@ -270,45 +335,25 @@
             term = term + pltpu.roll(term, shift, 1)
         start = M + i * D
         block = jnp.where((lane >= start) & (lane < start + D), term * owner, block)
-    grad_src[3 * W : 3 * W + D, :] = block
-    pick_heads = jnp.where(iota((S, W), 0) // M == iota((S, W), 1), 1.0, 0.0)
+    late_src[W : W + D, :] = block
+    pick_heads = jnp.where(iota((S, W), 0) // M == iota((S, W), 1), 1.0, 0.0).astype(BF16)
     temp = jnp.sum(dot32(temp_acc[...] * -inv_s, pick_heads), axis=0, keepdims=True)
     bias = jnp.sum(bias_acc[...], axis=0, keepdims=True)
     row = iota((8, W), 0)
-    grad_src[3 * W + D : 3 * W + D + 8, :] = jnp.where(row == 0, bias, jnp.where(row == 1, temp, 0.0))
-    used = 3 * W + D + 8
-    if used < parts * part_rows:
-        grad_src[used:, :] = jnp.zeros((parts * part_rows - used, W), F32)
-
-    def part(ref, p):
-        return ref.at[pl.ds(pl.multiple_of(p * part_rows, 8), part_rows), :]
-
-    copies = [
-        send(part(grad_src, group_peer(k)), grad_recv.at[k - 1], d_send.at[k - 1], d_recv.at[k - 1], group_id(k))
-        for k in range(1, parts)
-    ]
-    total = part(grad_src, group)[...]
-    for k, copy in enumerate(copies):
+    late_src[W + D : W + D + 8, :] = jnp.where(row == 0, bias, jnp.where(row == 1, temp, 0.0))
+    used = W + D + 8
+    if used < parts * late_rows:
+        late_src[used:, :] = jnp.zeros((parts * late_rows - used, W), F32)
+
+    late = start_scatter(late_src, late_recv, late_rows, late_sems)
+    late = start_across(late, late_src, late_recv, late_z, late_rows, late_sems)
+    late = start_gather(late, late_z, late_full, late_rows, late_sems)
+    for copy in early:
         copy.wait()
-        total = total + grad_recv[k]
-    grad_z[high] = total
-    copies = [
-        send(grad_z.at[high], grad_z.at[high], e_send.at[k - 1], e_recv.at[k - 1], high_id(k))
-        for k in range(1, high_n)
-    ]
-    for copy in copies:
+    packed_ref[0 : 2 * W, :] = early_full[...]
+    for copy in late:
         copy.wait()
-    total = grad_z[0]
-    for k in range(1, high_n):
-        total = total + grad_z[k]
-    mine = part(grad_full, group)
-    mine[...] = total
-    copies = [
-        send(mine, mine, f_send.at[k - 1], f_recv.at[k - 1], group_id(k)) for k in range(1, parts)
-    ]
-    for copy in copies:
-        copy.wait()
-    packed_ref[...] = grad_full[...]
+    packed_ref[2 * W :, :] = late_full[...]
     store_mf.wait()
 
 
@@ -321,9 +366,9 @@
 
     @pl.when(pl.program_id(0) == 0)
     def _():
-        mid_ref[...] = packed_ref[0:W, :]
-        feature_ref[...] = packed_ref[W : 2 * W, :]
-        proj_ref[...] = packed_ref[2 * W : 3 * W, :]
+        feature_ref[...] = packed_ref[0:W, :]
+        proj_ref[...] = packed_ref[W : 2 * W, :]
+        mid_ref[...] = packed_ref[2 * W : 3 * W, :]
         block = packed_ref[3 * W : 3 * W + D, :]
         slice_ref[...] = block[:, 0:M]
         query_ref[...] = block[:, M : M + D]
@@ -338,16 +383,18 @@
     rows = x.shape[0]
     high_n = n_node // LOW
     parts = n_member * LOW
-    used = 3 * W + D + 8
-    part_rows = -(-used // (8 * parts)) * 8
+    early_rows = -(-2 * W // (8 * parts)) * 8
+    late_rows = -(-(W + D + 8) // (8 * parts)) * 8
+    packed_rows = 2 * W + parts * late_rows
+    assert parts * early_rows == 2 * W and n_node % LOW == 0
     vmem = pl.BlockSpec(memory_space=pltpu.VMEM)
     hbm = pl.BlockSpec(memory_space=pl.ANY)
     dma = pltpu.SemaphoreType.DMA
     flops = 2 * rows * S * S * 12
     packed, mf = pl.pallas_call(
-        functools.partial(main_kernel, n_member, n_node, parts, part_rows),
+        functools.partial(main_kernel, n_member, n_node, parts, early_rows, late_rows),
         out_shape=(
-            jax.ShapeDtypeStruct((parts * part_rows, W), F32),
+            jax.ShapeDtypeStruct((packed_rows, W), F32),
             jax.ShapeDtypeStruct((rows, 2 * W), BF16),
         ),
         in_specs=[pl.BlockSpec(memory_space=pltpu.SMEM), hbm, hbm] + [vmem] * 8,
@@ -361,9 +408,13 @@
             pltpu.VMEM((rows, S), F32),
             pltpu.VMEM((rows, S), F32),
             pltpu.VMEM((rows, 2 * W), BF16),
+            pltpu.VMEM((rows // CHUNK, W, CHUNK), BF16),
+            pltpu.VMEM((rows // CHUNK, W, CHUNK), BF16),
+            pltpu.VMEM((rows // CHUNK, W, CHUNK), BF16),
             pltpu.VMEM((S, 2 * W), F32),
             pltpu.VMEM((8, S), F32),
-            pltpu.VMEM((W, 2 * W), F32),
+            pltpu.VMEM((W, W), F32),
+            pltpu.VMEM((W, W), F32),
             pltpu.VMEM((W, S), F32),
             pltpu.VMEM((W, W), F32),
             pltpu.VMEM((8, W), F32),
@@ -372,21 +423,24 @@
             pltpu.VMEM((LOW - 1, 24, W), F32),
             pltpu.VMEM((high_n, 24, W), F32),
             pltpu.VMEM((LOW, 24, W), F32),
-            pltpu.VMEM((parts * part_rows, W), F32),
-            pltpu.VMEM((parts - 1, part_rows, W), F32),
-            pltpu.VMEM((high_n, part_rows, W), F32),
-            pltpu.VMEM((parts * part_rows, W), F32),
+            pltpu.VMEM((parts * early_rows, W), F32),
+            pltpu.VMEM((parts - 1, early_rows, W), F32),
+            pltpu.VMEM((high_n, early_rows, W), F32),
+            pltpu.VMEM((parts * early_rows, W), F32),
+            pltpu.VMEM((parts * late_rows, W), F32),
+            pltpu.VMEM((parts - 1, late_rows, W), F32),
+            pltpu.VMEM((high_n, late_rows, W), F32),
+            pltpu.VMEM((parts * late_rows, W), F32),
             dma((2,)),
             dma,
             dma((LOW - 1,)), dma((LOW - 1,)),
             dma((high_n - 1,)), dma((high_n - 1,)),
             dma((LOW - 1,)), dma((LOW - 1,)),
-            dma((parts - 1,)), dma((parts - 1,)),
-            dma((high_n - 1,)), dma((high_n - 1,)),
-            dma((parts - 1,)), dma((parts - 1,)),
+            dma((6, max(parts, high_n) - 1)),
+            dma((6, max(parts, high_n) - 1)),
         ],
         compiler_params=pltpu.CompilerParams(
-            collective_id=0, has_side_effects=True, vmem_limit_bytes=48 * 1024 * 1024
+            collective_id=0, has_side_effects=True, vmem_limit_bytes=VMEM_LIMIT
         ),
         cost_estimate=pl.CostEstimate(
             flops=flops, bytes_accessed=rows * W * 8, transcendentals=rows * S
@@ -412,7 +466,7 @@
             jax.ShapeDtypeStruct((W, W), F32),
         ),
         in_specs=[
-            whole(parts * part_rows, W),
+            whole(packed_rows, W),
             pl.BlockSpec((tile, 2 * W), lambda i: (i, 0)),
             whole(W, W),
             whole(W, W),
@@ -422,7 +476,7 @@
             whole(W, W), whole(W, W), whole(1, W), whole(D, M), whole(1, HEADS),
             whole(D, D), whole(D, D), whole(D, D), whole(W, W),
         ),
-        compiler_params=pltpu.CompilerParams(vmem_limit_bytes=32 * 1024 * 1024),
+        compiler_params=pltpu.CompilerParams(vmem_limit_bytes=VMEM_LIMIT),
         cost_estimate=pl.CostEstimate(
             flops=2 * rows * 2 * W * W, bytes_accessed=rows * W * 8, transcendentals=0
         ),

time: 59.2 us -> 54.1 us (0.914)
  local copies, waits for them, and re-layouts: 8.77 us -> 0 us
  Pallas kernels: 49.3 us -> 53.1 us
    unnamed x22 -> x0, local copies, waits for them, and re-layouts: 8.77 us -> none
    pallas_call x1, Pallas kernels: 46.6 us -> 48.6 us  [shards(): pl.pallas_call(functools.partial(main_kernel, n_member, n_node, parts, ea...]
    pallas_call x1, Pallas kernels: 2.65 us -> 4.53 us  [shards(): pl.pallas_call(final_kernel, grid=(rows // tile,), out_shape=(jax.ShapeDt...]
where the time goes in v2:
time: 54.1 us; the launch traced here: 53.8 us
  Pallas kernels  53.1 us (98%)
  between operations  0.65 us (1%)
    pallas_call x1, Pallas kernels, shards(): pl.pallas_call(functools.partial(main_kernel, n_member, n_node, parts, ea...  48.6 us
    pallas_call x1, Pallas kernels, shards(): pl.pallas_call(final_kernel, grid=(rows // tile,), out_shape=(jax.ShapeDt...  4.53 us

profile of v2, /device:TPU:0, one launch (start us, length us, event | category | flops | bytes accessed | tf_op | source)
XLA Modules:
  0.0 53.8 jit_solution(210143420047181229)
XLA Ops:
  0.6 48.6 %pool_and_gradients.1 = (f32[448,128]{1,0:T(8,128)}, bf16[4096,256]{1,0:T(8,128)(2,1)}) custom-call(f32[8]{0:T(128)} %s_ref.1, bf16[4096,128]{1,0:T(8,128)(2,1)} %bitcast.7, bf16[4096,128]{1,0:T(8,128)(2,1)} %bitcast.8, bf16[128,128]{1,0:T(8,128)(2,1)} %w1_ref.3, bf16[128,128]{1,0:T(8,128)(2,1)} %w2_ref.3, f32[1,128]{1,0:T(1,128)} %bitcast.9, ...), custom_call_target="tpu_custom_call" | custom-call | flops 6442450944 | bytes 4194304 | tf_op jit(solution)/shard_map/pool_and_gradients/pallas_call | solution.py:394
  49.2 4.5 %vertex_and_unpack.1 = (f32[4096,128]{1,0:T(8,128)}, f32[128,128]{1,0:T(8,128)}, f32[128,128]{1,0:T(8,128)}, f32[1,128]{1,0:T(1,128)}, f32[16,32]{1,0:T(8,128)},...) custom-call(f32[448,128]{1,0:T(8,128)} %get-tuple-element.22.packed_ref, ...), custom_call_target="tpu_custom_call" | custom-call | flops 268435456 | bytes 4194304 | tf_op jit(solution)/shard_map/vertex_and_unpack/pallas_call | solution.py:453

commit v3 on v2

--- a/solution.py
+++ b/solution.py
@@ -14,8 +14,9 @@
 D = 16
 S = HEADS * M
 LOW = 4
-CHUNK = 512
+CHUNK = 1024
 EPS = 1e-05
+PIECES = 4
 VMEM_LIMIT = 62 * 1024 * 1024
 F32 = jnp.float32
 BF16 = jnp.bfloat16
@@ -50,8 +51,12 @@
     return lax.broadcasted_iota(jnp.int32, shape, axis)
 
 
+def block_of(index, size):
+    return index >> (size.bit_length() - 1)
+
+
 def group_sum(values, ones):
-    return dot32(values, ones)
+    return dot(jnp.concatenate(split(values), axis=1), ones)
 
 
 def fold_rows(a, step):
@@ -64,8 +69,8 @@
 def main_kernel(
     n_member, n_node, parts, early_rows, late_rows,
     s_ref, x_hbm, g_hbm, w1_ref, w2_ref, off_ref, a_ref, wq_ref, wk_ref, wv_ref, w3_ref,
-    packed_ref, mf_hbm,
-    x_ref, g_ref, mid_ref, fb_ref, pb_ref, probs_ref, logits_ref, mf_ref,
+    packed_ref, vertex_hbm,
+    x_ref, g_ref, mid_ref, fb_ref, pb_ref, probs_ref, logits_ref, mf_ref, vertex_ref,
     xt_ref, gt_ref, midt_ref,
     pool_acc, den_acc, mid_acc, feature_acc, slice_acc, proj_acc, bias_acc, temp_acc,
     pool_src, pool_recv, pool_z, pool_full,
@@ -99,10 +104,16 @@
         peer = group_peer(k)
         return (lax.div(peer, LOW), high * LOW + lax.rem(peer, LOW))
 
-    load_x = pltpu.make_async_copy(x_hbm, x_ref, in_sem.at[0])
-    load_g = pltpu.make_async_copy(g_hbm, g_ref, in_sem.at[1])
-    load_x.start()
-    load_g.start()
+    def load(i):
+        at = pl.ds(pl.multiple_of(i * CHUNK, CHUNK), CHUNK)
+        return (
+            pltpu.make_async_copy(x_hbm.at[at, :], x_ref.at[at, :], in_sem.at[0, i]),
+            pltpu.make_async_copy(g_hbm.at[at, :], g_ref.at[at, :], in_sem.at[1, i]),
+        )
+
+    for i in range(rows // CHUNK):
+        for copy in load(i):
+            copy.start()
 
     barrier = pltpu.get_barrier_semaphore()
     for k in range(1, parts):
@@ -118,18 +129,20 @@
         copy.start()
         return copy
 
-    head_of_slice = iota((1, S), 1) // M
+    head_of_slice = block_of(iota((1, S), 1), M)
     inv_s = jnp.zeros((1, S), F32)
     for h in range(HEADS):
         inv_s = jnp.where(head_of_slice == h, 1.0 / jnp.full((1, S), s_ref[h], F32), inv_s)
-    ones = jnp.where(iota((S, S), 0) // M == iota((S, S), 1) // M, 1.0, 0.0).astype(BF16)
-    same_head = iota((W, S), 0) // D == iota((W, S), 1) // M
-    pick_rows = jnp.where(iota((W, D), 0) % D == iota((W, D), 1), 1.0, 0.0).astype(BF16)
-    pick_slices = jnp.where(iota((M, S), 1) % M == iota((M, S), 0), 1.0, 0.0).astype(BF16)
-    pick_columns = jnp.where(iota((D, W), 1) % D == iota((D, W), 0), 1.0, 0.0).astype(BF16)
+    inside = block_of(iota((S, S), 0), M) == block_of(iota((S, S), 1), M)
+    ones = jnp.where(inside, 1.0, 0.0).astype(BF16)
+    ones = jnp.concatenate([ones, ones], axis=0)
+    same_head = block_of(iota((W, S), 0), D) == block_of(iota((W, S), 1), M)
+    pick_rows = jnp.where((iota((W, D), 0) & (D - 1)) == iota((W, D), 1), 1.0, 0.0).astype(BF16)
+    pick_slices = jnp.where((iota((M, S), 1) & (M - 1)) == iota((M, S), 0), 1.0, 0.0).astype(BF16)
+    pick_columns = jnp.where((iota((D, W), 1) & (D - 1)) == iota((D, W), 0), 1.0, 0.0).astype(BF16)
     a_all = dot(dot(pick_rows, a_ref[...]).astype(BF16), pick_slices)
     a_block = jnp.where(same_head, a_all, 0.0).astype(BF16)
-    head_square = iota((W, W), 0) // D == iota((W, W), 1) // D
+    head_square = block_of(iota((W, W), 0), D) == block_of(iota((W, W), 1), D)
 
     def square_block(ref):
         return jnp.where(
@@ -142,10 +155,10 @@
 
     pool_acc[...] = jnp.zeros_like(pool_acc)
     den_acc[...] = jnp.zeros_like(den_acc)
-    load_x.wait()
-    load_g.wait()
 
     def first(i, carry):
+        for copy in load(i):
+            copy.wait()
         at = pl.ds(pl.multiple_of(i * CHUNK, CHUNK), CHUNK)
         x = x_ref[at, :]
         both = dot(x, w12)
@@ -154,7 +167,9 @@
         back = dot(g_ref[at, :], w3, NT).astype(BF16)
         logits = dot(mid, a_block) * inv_s
         e = jnp.exp(logits)
-        probs = e / group_sum(e, ones)
+        total = group_sum(e, ones)
+        guess = pl.reciprocal(total, approx=True)
+        probs = e * (guess * (2.0 - total * guess))
         pb = probs.astype(BF16)
         fb = jnp.concatenate([back, feat], axis=1)
         mid_ref[at, :] = mid
@@ -168,7 +183,7 @@
 
     lax.fori_loop(0, rows // CHUNK, first, 0)
 
-    slice_head = iota((S, W), 0) // M == iota((S, W), 1) // D
+    slice_head = block_of(iota((S, W), 0), M) == block_of(iota((S, W), 1), D)
     token_grad = fold_rows(jnp.where(slice_head, pool_acc[:, :W], 0.0), M)
     numer = fold_rows(jnp.where(slice_head, pool_acc[:, W:], 0.0), M)
     den = jnp.sum(den_acc[...], axis=0, keepdims=True)
@@ -229,7 +244,6 @@
     maps = jnp.concatenate([square_block(r) for r in (wq_ref, wk_ref, wv_ref)], axis=1)
     qkv = dot32(tokens, maps)
     q, k, v = qkv[:, :W], qkv[:, W : 2 * W], qkv[:, 2 * W :]
-    inside = iota((S, S), 0) // M == iota((S, S), 1) // M
     scale = 1.0 / math.sqrt(D)
     scores = jnp.where(inside, dot32(q, k, NT) * scale, 0.0)
     e = jnp.where(inside, jnp.exp(scores), 0.0)
@@ -317,8 +331,6 @@
     lax.fori_loop(0, steps // 2, third, 0)
     early = start_across(early, early_src, early_recv, early_z, early_rows, early_sems)
     lax.fori_loop(steps // 2, steps, third, 0)
-    store_mf = pltpu.make_async_copy(mf_ref, mf_hbm, out_sem)
-    store_mf.start()
     early = start_gather(early, early_z, early_full, early_rows, early_sems)
 
     late_src[0:W, :] = mid_acc[...]
@@ -336,7 +348,7 @@
         start = M + i * D
         block = jnp.where((lane >= start) & (lane < start + D), term * owner, block)
     late_src[W : W + D, :] = block
-    pick_heads = jnp.where(iota((S, W), 0) // M == iota((S, W), 1), 1.0, 0.0).astype(BF16)
+    pick_heads = jnp.where(block_of(iota((S, W), 0), M) == iota((S, W), 1), 1.0, 0.0).astype(BF16)
     temp = jnp.sum(dot32(temp_acc[...] * -inv_s, pick_heads), axis=0, keepdims=True)
     bias = jnp.sum(bias_acc[...], axis=0, keepdims=True)
     row = iota((8, W), 0)
@@ -346,7 +358,20 @@
         late_src[used:, :] = jnp.zeros((parts * late_rows - used, W), F32)
 
     late = start_scatter(late_src, late_recv, late_rows, late_sems)
+
+    def store(i):
+        at = pl.ds(pl.multiple_of(i * CHUNK, CHUNK), CHUNK)
+        return pltpu.make_async_copy(vertex_ref.at[at, :], vertex_hbm.at[at, :], out_sem.at[i])
+
+    def fourth(i, carry):
+        at = pl.ds(pl.multiple_of(i * CHUNK, CHUNK), CHUNK)
+        vertex_ref[at, :] = dot(mf_ref[at, :], w12, NT)
+        store(i).start()
+        return carry
+
+    lax.fori_loop(0, steps // 2, fourth, 0)
     late = start_across(late, late_src, late_recv, late_z, late_rows, late_sems)
+    lax.fori_loop(steps // 2, steps, fourth, 0)
     late = start_gather(late, late_z, late_full, late_rows, late_sems)
     for copy in early:
         copy.wait()
@@ -354,28 +379,36 @@
     for copy in late:
         copy.wait()
     packed_ref[2 * W :, :] = late_full[...]
-    store_mf.wait()
+    for i in range(steps):
+        store(i).wait()
 
 
 def final_kernel(
-    packed_ref, mf_ref, w1_ref, w2_ref,
+    packed_ref, vertex_ref,
     out_ref, mid_ref, feature_ref, bias_ref, slice_ref, temp_ref, query_ref, key_ref, value_ref, proj_ref,
+    sems,
 ):
-    w12 = jnp.concatenate([w1_ref[...], w2_ref[...]], axis=1)
-    out_ref[...] = dot(mf_ref[...], w12, NT)
-
-    @pl.when(pl.program_id(0) == 0)
-    def _():
-        feature_ref[...] = packed_ref[0:W, :]
-        proj_ref[...] = packed_ref[W : 2 * W, :]
-        mid_ref[...] = packed_ref[2 * W : 3 * W, :]
-        block = packed_ref[3 * W : 3 * W + D, :]
-        slice_ref[...] = block[:, 0:M]
-        query_ref[...] = block[:, M : M + D]
-        key_ref[...] = block[:, M + D : M + 2 * D]
-        value_ref[...] = block[:, M + 2 * D : M + 3 * D]
-        bias_ref[...] = packed_ref[3 * W + D : 3 * W + D + 1, :]
-        temp_ref[...] = packed_ref[3 * W + D + 1 : 3 * W + D + 2, 0:HEADS]
+    size = vertex_ref.shape[0] // PIECES
+    copies = [
+        pltpu.make_async_copy(
+            vertex_ref.at[pl.ds(i * size, size), :], out_ref.at[pl.ds(i * size, size), :], sems.at[i]
+        )
+        for i in range(PIECES)
+    ]
+    for copy in copies:
+        copy.start()
+    feature_ref[...] = packed_ref[0:W, :]
+    proj_ref[...] = packed_ref[W : 2 * W, :]
+    mid_ref[...] = packed_ref[2 * W : 3 * W, :]
+    block = packed_ref[3 * W : 3 * W + D, :]
+    slice_ref[...] = block[:, 0:M]
+    query_ref[...] = block[:, M : M + D]
+    key_ref[...] = block[:, M + D : M + 2 * D]
+    value_ref[...] = block[:, M + 2 * D : M + 3 * D]
+    bias_ref[...] = packed_ref[3 * W + D : 3 * W + D + 1, :]
+    temp_ref[...] = packed_ref[3 * W + D + 1 : 3 * W + D + 2, 0:HEADS]
+    for copy in copies:
+        copy.wait()
 
 
 def shards(n_member, n_node, x, g, w1, w2, offset, a, s, wq, wk, wv, w3):
@@ -391,11 +424,11 @@
     hbm = pl.BlockSpec(memory_space=pl.ANY)
     dma = pltpu.SemaphoreType.DMA
     flops = 2 * rows * S * S * 12
-    packed, mf = pl.pallas_call(
+    packed, vertex = pl.pallas_call(
         functools.partial(main_kernel, n_member, n_node, parts, early_rows, late_rows),
         out_shape=(
             jax.ShapeDtypeStruct((packed_rows, W), F32),
-            jax.ShapeDtypeStruct((rows, 2 * W), BF16),
+            jax.ShapeDtypeStruct((rows, W), F32),
         ),
         in_specs=[pl.BlockSpec(memory_space=pltpu.SMEM), hbm, hbm] + [vmem] * 8,
         out_specs=(vmem, hbm),
@@ -408,6 +441,7 @@
             pltpu.VMEM((rows, S), F32),
             pltpu.VMEM((rows, S), F32),
             pltpu.VMEM((rows, 2 * W), BF16),
+            pltpu.VMEM((rows, W), F32),
             pltpu.VMEM((rows // CHUNK, W, CHUNK), BF16),
             pltpu.VMEM((rows // CHUNK, W, CHUNK), BF16),
             pltpu.VMEM((rows // CHUNK, W, CHUNK), BF16),
@@ -431,8 +465,8 @@
             pltpu.VMEM((parts - 1, late_rows, W), F32),
             pltpu.VMEM((high_n, late_rows, W), F32),
             pltpu.VMEM((parts * late_rows, W), F32),
-            dma((2,)),
-            dma,
+            dma((2, rows // CHUNK)),
+            dma((rows // CHUNK,)),
             dma((LOW - 1,)), dma((LOW - 1,)),
             dma((high_n - 1,)), dma((high_n - 1,)),
             dma((LOW - 1,)), dma((LOW - 1,)),
@@ -448,11 +482,8 @@
         name="pool_and_gradients",
     )(s, x, g, w1, w2, offset.reshape(1, W), a, wq, wk, wv, w3)
 
-    tile = 1024
-    whole = lambda *shape: pl.BlockSpec(shape, lambda i: (0,) * len(shape))
     outs = pl.pallas_call(
         final_kernel,
-        grid=(rows // tile,),
         out_shape=(
             jax.ShapeDtypeStruct((rows, W), F32),
             jax.ShapeDtypeStruct((W, W), F32),
@@ -465,23 +496,13 @@
             jax.ShapeDtypeStruct((D, D), F32),
             jax.ShapeDtypeStruct((W, W), F32),
         ),
-        in_specs=[
-            whole(packed_rows, W),
-            pl.BlockSpec((tile, 2 * W), lambda i: (i, 0)),
-            whole(W, W),
-            whole(W, W),
-        ],
-        out_specs=(
-            pl.BlockSpec((tile, W), lambda i: (i, 0)),
-            whole(W, W), whole(W, W), whole(1, W), whole(D, M), whole(1, HEADS),
-            whole(D, D), whole(D, D), whole(D, D), whole(W, W),
-        ),
+        in_specs=[vmem, hbm],
+        out_specs=(hbm,) + (vmem,) * 9,
+        scratch_shapes=[dma((PIECES,))],
         compiler_params=pltpu.CompilerParams(vmem_limit_bytes=VMEM_LIMIT),
-        cost_estimate=pl.CostEstimate(
-            flops=2 * rows * 2 * W * W, bytes_accessed=rows * W * 8, transcendentals=0
-        ),
-        name="vertex_and_unpack",
-    )(packed, mf, w1, w2)
+        cost_estimate=pl.CostEstimate(flops=0, bytes_accessed=rows * W * 8, transcendentals=0),
+        name="unpack",
+    )(packed, vertex)
     vertex, mid, feature, bias, slices, temp, query, key, value, proj = outs
     return (
         vertex[None], mid, feature, bias.reshape(W), slices, temp.reshape(HEADS),

time: 54.1 us -> 112 us (2.07)
  Pallas kernels: 53.1 us -> 111 us
    pallas_call x1, Pallas kernels: 4.53 us -> 66.3 us  [shards(): pl.pallas_call(final_kernel, out_shape=(jax.ShapeDtypeStruct((rows, W), F...]
    pallas_call x1, Pallas kernels: 48.6 us -> 44.9 us  [shards(): pl.pallas_call(functools.partial(main_kernel, n_member, n_node, parts, ea...]
where the time goes in v3:
time: 112 us
  Pallas kernels  111 us (99%)
    pallas_call x1, Pallas kernels, shards(): pl.pallas_call(final_kernel, out_shape=(jax.ShapeDtypeStruct((rows, W), F...  66.3 us
    pallas_call x1, Pallas kernels, shards(): pl.pallas_call(functools.partial(main_kernel, n_member, n_node, parts, ea...  44.9 us

profile of v3, /device:TPU:0, one launch (start us, length us, event | category | flops | bytes accessed | tf_op | source)
XLA Modules:
  0.0 111.9 jit_solution(9873967291368720052)
XLA Ops:
  0.6 44.9 %pool_and_gradients.1 = (f32[448,128]{1,0:T(8,128)}, f32[4096,128]{1,0:T(8,128)}) custom-call(f32[8]{0:T(128)} %s_ref.1, bf16[4096,128]{1,0:T(8,128)(2,1)} %bitcast.7, bf16[4096,128]{1,0:T(8,128)(2,1)} %bitcast.8, bf16[128,128]{1,0:T(8,128)(2,1)} %w1_ref.1, bf16[128,128]{1,0:T(8,128)(2,1)} %w2_ref.1, f32[1,128]{1,0:T(1,128)} %bitcast.9, ...), custom_call_target="tpu_custom_call" | custom-call | flops 6442450944 | bytes 4194304 | tf_op jit(solution)/shard_map/pool_and_gradients/pallas_call | solution.py:427
  45.6 66.3 %unpack.1 = (f32[4096,128]{1,0:T(8,128)}, f32[128,128]{1,0:T(8,128)}, f32[128,128]{1,0:T(8,128)}, f32[1,128]{1,0:T(1,128)}, f32[16,32]{1,0:T(8,128)}, /*index=5*...) custom-call(f32[448,128]{1,0:T(8,128)} %get-tuple-element.22.packed_ref, ...), custom_call_target="tpu_custom_call" | custom-call | bytes 4194304 | tf_op jit(solution)/shard_map/unpack/pallas_call | solution.py:485

commit v4 on v3

--- a/solution.py
+++ b/solution.py
@@ -14,9 +14,9 @@
 D = 16
 S = HEADS * M
 LOW = 4
-CHUNK = 1024
+CHUNK = 2048
 EPS = 1e-05
-PIECES = 4
+PIECES = 8
 VMEM_LIMIT = 62 * 1024 * 1024
 F32 = jnp.float32
 BF16 = jnp.bfloat16
@@ -149,8 +149,12 @@
             head_square, dot(dot(pick_rows, ref[...]).astype(BF16), pick_columns), 0.0
         ).astype(BF16)
 
+    maps = jnp.concatenate([square_block(r) for r in (wq_ref, wk_ref, wv_ref)], axis=1)
+    maps_back = maps.T
     w12 = jnp.concatenate([w1_ref[...], w2_ref[...]], axis=1)
-    w3 = w3_ref[...]
+    w12_back = w12.T
+    w3_back = w3_ref[...].T
+    a_back = a_block.T
     offset = off_ref[...]
 
     pool_acc[...] = jnp.zeros_like(pool_acc)
@@ -164,7 +168,7 @@
         both = dot(x, w12)
         mid = both[:, :W].astype(BF16)
         feat = (both[:, W:] + offset).astype(BF16)
-        back = dot(g_ref[at, :], w3, NT).astype(BF16)
+        back = dot(g_ref[at, :], w3_back).astype(BF16)
         logits = dot(mid, a_block) * inv_s
         e = jnp.exp(logits)
         total = group_sum(e, ones)
@@ -241,7 +245,6 @@
     numer = jnp.where(slice_head, jnp.concatenate([numer] * HEADS, axis=0), 0.0)
     token_grad = jnp.where(slice_head, jnp.concatenate([token_grad] * HEADS, axis=0), 0.0)
     tokens = numer / (den + EPS)
-    maps = jnp.concatenate([square_block(r) for r in (wq_ref, wk_ref, wv_ref)], axis=1)
     qkv = dot32(tokens, maps)
     q, k, v = qkv[:, :W], qkv[:, W : 2 * W], qkv[:, 2 * W :]
     scale = 1.0 / math.sqrt(D)
@@ -254,12 +257,13 @@
     d_qkv = jnp.concatenate(
         [dot32(d_scores, k), dot32(d_scores, q, TN), dot32(share, token_grad, TN)], axis=1
     )
-    tok_back = dot32(d_qkv, maps, NT)
+    tok_back = dot32(d_qkv, maps_back)
     numer_back = (tok_back * inverse).astype(BF16)
     den_back = -jnp.sum(tok_back * tokens, axis=1, keepdims=True) * inverse
     den_back = jnp.sum(jnp.where(eye, den_back, 0.0), axis=0, keepdims=True)
     d_maps = dot32(tokens, d_qkv, TN)
     mix = jnp.concatenate([token_out, numer_back], axis=1)
+    mix_back = mix.T
 
     for acc in (mid_acc, feature_acc, slice_acc, proj_acc, bias_acc, temp_acc):
         acc[...] = jnp.zeros_like(acc)
@@ -312,12 +316,12 @@
     def third(i, carry):
         at = pl.ds(pl.multiple_of(i * CHUNK, CHUNK), CHUNK)
         probs = probs_ref[at, :]
-        prob_back = dot(fb_ref[at, :], mix, NT) + den_back
+        prob_back = dot(fb_ref[at, :], mix_back) + den_back
         inner = group_sum(probs * prob_back, ones)
         logit_back = probs * (prob_back - inner)
         temp_acc[...] += jnp.sum((logit_back * logits_ref[at, :]).reshape(CHUNK // 8, 8, S), axis=0)
         score_back = (logit_back * inv_s).astype(BF16)
-        mid_back = dot(score_back, a_block, NT).astype(BF16)
+        mid_back = dot(score_back, a_back).astype(BF16)
         mf_ref[at, :W] = mid_back
         mid_acc[...] += dot(xt_ref[i], mid_back)
         slice_acc[...] += dot(midt_ref[i], score_back)
@@ -365,7 +369,7 @@
 
     def fourth(i, carry):
         at = pl.ds(pl.multiple_of(i * CHUNK, CHUNK), CHUNK)
-        vertex_ref[at, :] = dot(mf_ref[at, :], w12, NT)
+        vertex_ref[at, :] = dot(mf_ref[at, :], w12_back)
         store(i).start()
         return carry
 
@@ -386,16 +390,22 @@
 def final_kernel(
     packed_ref, vertex_ref,
     out_ref, mid_ref, feature_ref, bias_ref, slice_ref, temp_ref, query_ref, key_ref, value_ref, proj_ref,
-    sems,
+    held, sems,
 ):
     size = vertex_ref.shape[0] // PIECES
+    pieces = [pl.ds(i * size, size) for i in range(PIECES)]
+    loads = [
+        pltpu.make_async_copy(vertex_ref.at[at, :], held.at[at, :], sems.at[0, i])
+        for i, at in enumerate(pieces)
+    ]
     copies = [
-        pltpu.make_async_copy(
-            vertex_ref.at[pl.ds(i * size, size), :], out_ref.at[pl.ds(i * size, size), :], sems.at[i]
-        )
-        for i in range(PIECES)
+        pltpu.make_async_copy(held.at[at, :], out_ref.at[at, :], sems.at[1, i])
+        for i, at in enumerate(pieces)
     ]
-    for copy in copies:
+    for copy in loads:
+        copy.start()
+    for before, copy in zip(loads, copies):
+        before.wait()
         copy.start()
     feature_ref[...] = packed_ref[0:W, :]
     proj_ref[...] = packed_ref[W : 2 * W, :]
@@ -498,7 +508,7 @@
         ),
         in_specs=[vmem, hbm],
         out_specs=(hbm,) + (vmem,) * 9,
-        scratch_shapes=[dma((PIECES,))],
+        scratch_shapes=[pltpu.VMEM((rows, W), F32), dma((2, PIECES))],
         compiler_params=pltpu.CompilerParams(vmem_limit_bytes=VMEM_LIMIT),
         cost_estimate=pl.CostEstimate(flops=0, bytes_accessed=rows * W * 8, transcendentals=0),
         name="unpack",

time: 112 us -> 48.4 us (0.43)
  Pallas kernels: 111 us -> 47.4 us
    pallas_call x1, Pallas kernels: 66.3 us -> 4.03 us  [shards(): pl.pallas_call(final_kernel, out_shape=(jax.ShapeDtypeStruct((rows, W), F...]
    pallas_call x1, Pallas kernels: 44.9 us -> 43.4 us  [shards(): pl.pallas_call(functools.partial(main_kernel, n_member, n_node, parts, ea...]
where the time goes in v4:
time: 48.4 us; the launch traced here: 48.1 us
  Pallas kernels  47.4 us (98%)
  between operations  0.65 us (1%)
    pallas_call x1, Pallas kernels, shards(): pl.pallas_call(functools.partial(main_kernel, n_member, n_node, parts, ea...  43.4 us
    pallas_call x1, Pallas kernels, shards(): pl.pallas_call(final_kernel, out_shape=(jax.ShapeDtypeStruct((rows, W), F...  4.03 us

profile of v4, /device:TPU:0, one launch (start us, length us, event | category | flops | bytes accessed | tf_op | source)
XLA Modules:
  0.0 48.1 jit_solution(8441128286066065889)
XLA Ops:
  0.6 43.4 %pool_and_gradients.1 = (f32[448,128]{1,0:T(8,128)}, f32[4096,128]{1,0:T(8,128)}) custom-call(f32[8]{0:T(128)} %s_ref.1, bf16[4096,128]{1,0:T(8,128)(2,1)} %bitcast.7, bf16[4096,128]{1,0:T(8,128)(2,1)} %bitcast.8, bf16[128,128]{1,0:T(8,128)(2,1)} %w1_ref.1, bf16[128,128]{1,0:T(8,128)(2,1)} %w2_ref.1, f32[1,128]{1,0:T(1,128)} %bitcast.9, ...), custom_call_target="tpu_custom_call" | custom-call | flops 6442450944 | bytes 4194304 | tf_op jit(solution)/shard_map/pool_and_gradients/pallas_call | solution.py:437
  44.0 4.0 %unpack.1 = (f32[4096,128]{1,0:T(8,128)}, f32[128,128]{1,0:T(8,128)}, f32[128,128]{1,0:T(8,128)}, f32[1,128]{1,0:T(1,128)}, f32[16,32]{1,0:T(8,128)}, /*index=5*...) custom-call(f32[448,128]{1,0:T(8,128)} %get-tuple-element.22.packed_ref, ...), custom_call_target="tpu_custom_call" | custom-call | bytes 4194304 | tf_op jit(solution)/shard_map/unpack/pallas_call | solution.py:495

commit v5 on v4

--- a/solution.py
+++ b/solution.py
@@ -71,8 +71,8 @@
     s_ref, x_hbm, g_hbm, w1_ref, w2_ref, off_ref, a_ref, wq_ref, wk_ref, wv_ref, w3_ref,
     packed_ref, vertex_hbm,
     x_ref, g_ref, mid_ref, fb_ref, pb_ref, probs_ref, logits_ref, mf_ref, vertex_ref,
-    xt_ref, gt_ref, midt_ref,
-    pool_acc, den_acc, mid_acc, feature_acc, slice_acc, proj_acc, bias_acc, temp_acc,
+    gxt_ref, midt_ref,
+    pool_acc, den_acc, mid_acc, second_acc, slice_acc, bias_acc, temp_acc,
     pool_src, pool_recv, pool_z, pool_full,
     early_src, early_recv, early_z, early_full, late_src, late_recv, late_z, late_full,
     in_sem, out_sem,
@@ -203,15 +203,15 @@
         send(pool_src.at[low_peer(k)], pool_recv.at[k - 1], a_send.at[k - 1], a_recv.at[k - 1], low_id(k))
         for k in range(1, LOW)
     ]
-    def turn(source, target):
+    def turn(source, target, start):
         def step(i, carry):
             at = pl.ds(pl.multiple_of(i * CHUNK, CHUNK), CHUNK)
-            target[i] = source[at, :].T
+            target[i, start : start + W, :] = source[at, :].T
             return carry
 
         lax.fori_loop(0, rows // CHUNK, step, 0)
 
-    turn(x_ref, xt_ref)
+    turn(x_ref, gxt_ref, W)
     total = pool_src[low]
     for k, copy in enumerate(copies):
         copy.wait()
@@ -221,8 +221,7 @@
         send(pool_z.at[high], pool_z.at[high], b_send.at[k - 1], b_recv.at[k - 1], high_id(k))
         for k in range(1, high_n)
     ]
-    turn(g_ref, gt_ref)
-    turn(mid_ref, midt_ref)
+    turn(g_ref, gxt_ref, 0)
     for copy in copies:
         copy.wait()
     total = pool_z[0]
@@ -233,6 +232,7 @@
         send(pool_full.at[low], pool_full.at[low], c_send.at[k - 1], c_recv.at[k - 1], low_id(k))
         for k in range(1, LOW)
     ]
+    turn(mid_ref, midt_ref, 0)
     for copy in copies:
         copy.wait()
 
@@ -265,7 +265,7 @@
     mix = jnp.concatenate([token_out, numer_back], axis=1)
     mix_back = mix.T
 
-    for acc in (mid_acc, feature_acc, slice_acc, proj_acc, bias_acc, temp_acc):
+    for acc in (mid_acc, second_acc, slice_acc, bias_acc, temp_acc):
         acc[...] = jnp.zeros_like(acc)
 
     def part(ref, p, size):
@@ -304,13 +304,11 @@
     def second(i, carry):
         at = pl.ds(pl.multiple_of(i * CHUNK, CHUNK), CHUNK)
         both = dot(pb_ref[at, :], mix)
-        mixed = both[:, :W].astype(BF16)
+        rounded = both.astype(BF16)
         feat_back = both[:, W:]
-        rounded = feat_back.astype(BF16)
-        mf_ref[at, W:] = rounded
+        mf_ref[at, W:] = rounded[:, W:]
         bias_acc[...] += jnp.sum(feat_back.reshape(CHUNK // 8, 8, W), axis=0)
-        proj_acc[...] += dot(gt_ref[i], mixed)
-        feature_acc[...] += dot(xt_ref[i], rounded)
+        second_acc[...] += dot(gxt_ref[i], rounded)
         return carry
 
     def third(i, carry):
@@ -323,14 +321,14 @@
         score_back = (logit_back * inv_s).astype(BF16)
         mid_back = dot(score_back, a_back).astype(BF16)
         mf_ref[at, :W] = mid_back
-        mid_acc[...] += dot(xt_ref[i], mid_back)
+        mid_acc[...] += dot(gxt_ref[i, W:, :], mid_back)
         slice_acc[...] += dot(midt_ref[i], score_back)
         return carry
 
     steps = rows // CHUNK
     lax.fori_loop(0, steps, second, 0)
-    early_src[0:W, :] = feature_acc[...]
-    early_src[W : 2 * W, :] = proj_acc[...].T
+    early_src[0:W, :] = second_acc[W:, W:]
+    early_src[W : 2 * W, :] = second_acc[:W, :W].T
     early = start_scatter(early_src, early_recv, early_rows, early_sems)
     lax.fori_loop(0, steps // 2, third, 0)
     early = start_across(early, early_src, early_recv, early_z, early_rows, early_sems)
@@ -390,34 +388,50 @@
 def final_kernel(
     packed_ref, vertex_ref,
     out_ref, mid_ref, feature_ref, bias_ref, slice_ref, temp_ref, query_ref, key_ref, value_ref, proj_ref,
-    held, sems,
+    packed, held, slice_out, query_out, key_out, value_out, load_sems, store_sems, small_sems,
 ):
     size = vertex_ref.shape[0] // PIECES
     pieces = [pl.ds(i * size, size) for i in range(PIECES)]
     loads = [
-        pltpu.make_async_copy(vertex_ref.at[at, :], held.at[at, :], sems.at[0, i])
+        pltpu.make_async_copy(vertex_ref.at[at, :], held.at[at, :], load_sems.at[i])
         for i, at in enumerate(pieces)
     ]
     copies = [
-        pltpu.make_async_copy(held.at[at, :], out_ref.at[at, :], sems.at[1, i])
+        pltpu.make_async_copy(held.at[at, :], out_ref.at[at, :], store_sems.at[i])
         for i, at in enumerate(pieces)
     ]
+    load_packed = pltpu.make_async_copy(packed_ref, packed, load_sems.at[PIECES])
+    load_packed.start()
     for copy in loads:
+        copy.start()
+    load_packed.wait()
+    block = packed[3 * W : 3 * W + D, :]
+    slice_out[...] = block[:, 0:M]
+    query_out[...] = block[:, M : M + D]
+    key_out[...] = block[:, M + D : M + 2 * D]
+    value_out[...] = block[:, M + 2 * D : M + 3 * D]
+    last = 3 * W + D
+    bias_ref[...] = packed[last : last + 1, :]
+    temp_ref[...] = packed[last + 1 : last + 2, 0:HEADS]
+    smalls = [
+        (packed.at[0:W, :], feature_ref),
+        (packed.at[W : 2 * W, :], proj_ref),
+        (packed.at[2 * W : 3 * W, :], mid_ref),
+        (slice_out, slice_ref),
+        (query_out, query_ref),
+        (key_out, key_ref),
+        (value_out, value_ref),
+    ]
+    smalls = [
+        pltpu.make_async_copy(source, target, small_sems.at[i])
+        for i, (source, target) in enumerate(smalls)
+    ]
+    for copy in smalls:
         copy.start()
     for before, copy in zip(loads, copies):
         before.wait()
         copy.start()
-    feature_ref[...] = packed_ref[0:W, :]
-    proj_ref[...] = packed_ref[W : 2 * W, :]
-    mid_ref[...] = packed_ref[2 * W : 3 * W, :]
-    block = packed_ref[3 * W : 3 * W + D, :]
-    slice_ref[...] = block[:, 0:M]
-    query_ref[...] = block[:, M : M + D]
-    key_ref[...] = block[:, M + D : M + 2 * D]
-    value_ref[...] = block[:, M + 2 * D : M + 3 * D]
-    bias_ref[...] = packed_ref[3 * W + D : 3 * W + D + 1, :]
-    temp_ref[...] = packed_ref[3 * W + D + 1 : 3 * W + D + 2, 0:HEADS]
-    for copy in copies:
+    for copy in smalls + copies:
         copy.wait()
 
 
@@ -452,15 +466,13 @@
             pltpu.VMEM((rows, S), F32),
             pltpu.VMEM((rows, 2 * W), BF16),
             pltpu.VMEM((rows, W), F32),
-            pltpu.VMEM((rows // CHUNK, W, CHUNK), BF16),
-            pltpu.VMEM((rows // CHUNK, W, CHUNK), BF16),
+            pltpu.VMEM((rows // CHUNK, 2 * W, CHUNK), BF16),
             pltpu.VMEM((rows // CHUNK, W, CHUNK), BF16),
             pltpu.VMEM((S, 2 * W), F32),
             pltpu.VMEM((8, S), F32),
             pltpu.VMEM((W, W), F32),
-            pltpu.VMEM((W, W), F32),
+            pltpu.VMEM((2 * W, 2 * W), F32),
             pltpu.VMEM((W, S), F32),
-            pltpu.VMEM((W, W), F32),
             pltpu.VMEM((8, W), F32),
             pltpu.VMEM((8, S), F32),
             pltpu.VMEM((LOW, 24, W), F32),
@@ -506,9 +518,17 @@
             jax.ShapeDtypeStruct((D, D), F32),
             jax.ShapeDtypeStruct((W, W), F32),
         ),
-        in_specs=[vmem, hbm],
-        out_specs=(hbm,) + (vmem,) * 9,
-        scratch_shapes=[pltpu.VMEM((rows, W), F32), dma((2, PIECES))],
+        in_specs=[hbm, hbm],
+        out_specs=(hbm, hbm, hbm, vmem, hbm, vmem, hbm, hbm, hbm, hbm),
+        scratch_shapes=[
+            pltpu.VMEM((packed_rows, W), F32),
+            pltpu.VMEM((rows, W), F32),
+            pltpu.VMEM((D, M), F32),
+            pltpu.VMEM((D, D), F32),
+            pltpu.VMEM((D, D), F32),
+            pltpu.VMEM((D, D), F32),
+            dma((PIECES + 1,)), dma((PIECES,)), dma((7,)),
+        ],
         compiler_params=pltpu.CompilerParams(vmem_limit_bytes=VMEM_LIMIT),
         cost_estimate=pl.CostEstimate(flops=0, bytes_accessed=rows * W * 8, transcendentals=0),
         name="unpack",

time: 48.4 us -> 46.9 us (0.969)
  Pallas kernels: 47.4 us -> 46 us
    pallas_call x1, Pallas kernels: 4.03 us -> 3.1 us  [shards(): pl.pallas_call(final_kernel, out_shape=(jax.ShapeDtypeStruct((rows, W), F...]
    pallas_call x1, Pallas kernels: 43.4 us -> 42.9 us  [shards(): pl.pallas_call(functools.partial(main_kernel, n_member, n_node, parts, ea...]
where the time goes in v5:
time: 46.9 us; the launch traced here: 46.7 us
  Pallas kernels  46 us (98%)
  between operations  0.65 us (1%)
    pallas_call x1, Pallas kernels, shards(): pl.pallas_call(functools.partial(main_kernel, n_member, n_node, parts, ea...  42.9 us
    pallas_call x1, Pallas kernels, shards(): pl.pallas_call(final_kernel, out_shape=(jax.ShapeDtypeStruct((rows, W), F...  3.1 us

profile of v5, /device:TPU:0, one launch (start us, length us, event | category | flops | bytes accessed | tf_op | source)
XLA Modules:
  0.0 46.7 jit_solution(8858973372677809935)
XLA Ops:
  0.6 42.9 %pool_and_gradients.1 = (f32[448,128]{1,0:T(8,128)}, f32[4096,128]{1,0:T(8,128)}) custom-call(f32[8]{0:T(128)} %s_ref.1, bf16[4096,128]{1,0:T(8,128)(2,1)} %bitcast.7, bf16[4096,128]{1,0:T(8,128)(2,1)} %bitcast.8, bf16[128,128]{1,0:T(8,128)(2,1)} %w1_ref.1, bf16[128,128]{1,0:T(8,128)(2,1)} %w2_ref.1, f32[1,128]{1,0:T(1,128)} %bitcast.9, ...), custom_call_target="tpu_custom_call" | custom-call | flops 6442450944 | bytes 4194304 | tf_op jit(solution)/shard_map/pool_and_gradients/pallas_call | solution.py:451
  43.6 3.1 %unpack.1 = (f32[4096,128]{1,0:T(8,128)}, f32[128,128]{1,0:T(8,128)}, f32[128,128]{1,0:T(8,128)}, f32[1,128]{1,0:T(1,128)}, f32[16,32]{1,0:T(8,128)}, /*index=5*...) custom-call(f32[448,128]{1,0:T(8,128)} %get-tuple-element.22.packed_ref, ...), custom_call_target="tpu_custom_call" | custom-call | bytes 4194304 | tf_op jit(solution)/shard_map/unpack/pallas_call | solution.py:507

commit v6 on v5

--- a/solution.py
+++ b/solution.py
@@ -70,9 +70,9 @@
     n_member, n_node, parts, early_rows, late_rows,
     s_ref, x_hbm, g_hbm, w1_ref, w2_ref, off_ref, a_ref, wq_ref, wk_ref, wv_ref, w3_ref,
     packed_ref, vertex_hbm,
-    x_ref, g_ref, mid_ref, fb_ref, pb_ref, probs_ref, logits_ref, mf_ref, vertex_ref,
+    x_ref, g_ref, mid_ref, fb_ref, pb_ref, probs_ref, mf_ref, vertex_ref,
     gxt_ref, midt_ref,
-    pool_acc, den_acc, mid_acc, second_acc, slice_acc, bias_acc, temp_acc,
+    pool_acc, den_acc, mid_acc, second_acc, slice_acc, bias_acc,
     pool_src, pool_recv, pool_z, pool_full,
     early_src, early_recv, early_z, early_full, late_src, late_recv, late_z, late_full,
     in_sem, out_sem,
@@ -180,7 +180,6 @@
         fb_ref[at, :] = fb
         pb_ref[at, :] = pb
         probs_ref[at, :] = probs
-        logits_ref[at, :] = logits
         pool_acc[...] += dot(pb, fb, TN)
         den_acc[...] += jnp.sum(probs.reshape(CHUNK // 8, 8, S), axis=0)
         return carry
@@ -265,7 +264,7 @@
     mix = jnp.concatenate([token_out, numer_back], axis=1)
     mix_back = mix.T
 
-    for acc in (mid_acc, second_acc, slice_acc, bias_acc, temp_acc):
+    for acc in (mid_acc, second_acc, slice_acc, bias_acc):
         acc[...] = jnp.zeros_like(acc)
 
     def part(ref, p, size):
@@ -317,7 +316,6 @@
         prob_back = dot(fb_ref[at, :], mix_back) + den_back
         inner = group_sum(probs * prob_back, ones)
         logit_back = probs * (prob_back - inner)
-        temp_acc[...] += jnp.sum((logit_back * logits_ref[at, :]).reshape(CHUNK // 8, 8, S), axis=0)
         score_back = (logit_back * inv_s).astype(BF16)
         mid_back = dot(score_back, a_back).astype(BF16)
         mf_ref[at, :W] = mid_back
@@ -336,7 +334,9 @@
     early = start_gather(early, early_z, early_full, early_rows, early_sems)
 
     late_src[0:W, :] = mid_acc[...]
-    slices = fold_rows(jnp.where(same_head, slice_acc[...], 0.0), D)
+    slices = jnp.where(same_head, slice_acc[...], 0.0)
+    temp = fold_rows(slices * a_block.astype(F32), 8) * -inv_s
+    slices = fold_rows(slices, D)
     slices = slices[:, :W] + slices[:, W:]
     slices = slices + pltpu.roll(slices, 64, 1)
     slices = slices + pltpu.roll(slices, 32, 1)
@@ -351,7 +351,7 @@
         block = jnp.where((lane >= start) & (lane < start + D), term * owner, block)
     late_src[W : W + D, :] = block
     pick_heads = jnp.where(block_of(iota((S, W), 0), M) == iota((S, W), 1), 1.0, 0.0).astype(BF16)
-    temp = jnp.sum(dot32(temp_acc[...] * -inv_s, pick_heads), axis=0, keepdims=True)
+    temp = jnp.sum(dot32(temp, pick_heads), axis=0, keepdims=True)
     bias = jnp.sum(bias_acc[...], axis=0, keepdims=True)
     row = iota((8, W), 0)
     late_src[W + D : W + D + 8, :] = jnp.where(row == 0, bias, jnp.where(row == 1, temp, 0.0))
@@ -463,7 +463,6 @@
             pltpu.VMEM((rows, 2 * W), BF16),
             pltpu.VMEM((rows, S), BF16),
             pltpu.VMEM((rows, S), F32),
-            pltpu.VMEM((rows, S), F32),
             pltpu.VMEM((rows, 2 * W), BF16),
             pltpu.VMEM((rows, W), F32),
             pltpu.VMEM((rows // CHUNK, 2 * W, CHUNK), BF16),
@@ -474,7 +473,6 @@
             pltpu.VMEM((2 * W, 2 * W), F32),
             pltpu.VMEM((W, S), F32),
             pltpu.VMEM((8, W), F32),
-            pltpu.VMEM((8, S), F32),
             pltpu.VMEM((LOW, 24, W), F32),
             pltpu.VMEM((LOW - 1, 24, W), F32),
             pltpu.VMEM((high_n, 24, W), F32),

time: 46.9 us -> 46.9 us (level)
  no operation moved by 1% of the time
where the time goes in v6:
time: 46.9 us; the launch traced here: 46.7 us
  Pallas kernels  46 us (98%)
  between operations  0.65 us (1%)
    pallas_call x1, Pallas kernels, shards(): pl.pallas_call(functools.partial(main_kernel, n_member, n_node, parts, ea...  42.9 us
    pallas_call x1, Pallas kernels, shards(): pl.pallas_call(final_kernel, out_shape=(jax.ShapeDtypeStruct((rows, W), F...  3.1 us

profile of v6, /device:TPU:0, one launch (start us, length us, event | category | flops | bytes accessed | tf_op | source)
XLA Modules:
  0.0 46.7 jit_solution(16647836724093807321)
XLA Ops:
  0.6 42.9 %pool_and_gradients.1 = (f32[448,128]{1,0:T(8,128)}, f32[4096,128]{1,0:T(8,128)}) custom-call(f32[8]{0:T(128)} %s_ref.1, bf16[4096,128]{1,0:T(8,128)(2,1)} %bitcast.7, bf16[4096,128]{1,0:T(8,128)(2,1)} %bitcast.8, bf16[128,128]{1,0:T(8,128)(2,1)} %w1_ref.1, bf16[128,128]{1,0:T(8,128)(2,1)} %w2_ref.1, f32[1,128]{1,0:T(1,128)} %bitcast.9, ...), custom_call_target="tpu_custom_call" | custom-call | flops 6442450944 | bytes 4194304 | tf_op jit(solution)/shard_map/pool_and_gradients/pallas_call | solution.py:451
  43.6 3.1 %unpack.1 = (f32[4096,128]{1,0:T(8,128)}, f32[128,128]{1,0:T(8,128)}, f32[128,128]{1,0:T(8,128)}, f32[1,128]{1,0:T(1,128)}, f32[16,32]{1,0:T(8,128)}, /*index=5*...) custom-call(f32[448,128]{1,0:T(8,128)} %get-tuple-element.22.packed_ref, ...), custom_call_target="tpu_custom_call" | custom-call | bytes 4194304 | tf_op jit(solution)/shard_map/unpack/pallas_call | solution.py:505
